TPU v7x, 128 devices: a whole 4x4x4 slice. The times are simulated.
128 devices in a mesh: seq: 16 (over y, x), patch: 8 (over z, core).
Axes of the slice: x: 4, y: 4, z: 4, core: 2. Of those that a mesh axis runs over, the one named last changes fastest.
Arguments:
- byte_states: bfloat16 [65536, 1024], P('seq'), may hold values from -16 to 16
- patch_len: int32 [16, 512], P('seq'), may hold values from 1 to 16, 4096 in all within a row
- shard_offset: int32 [16], P('seq'), may hold values from 0 to 15
- owner: int32 [16, 512], P('seq'), may hold values from 0 to 511, each once within a row
- cotangent: bfloat16 [8192, 4096], P('seq', 'patch'), may hold values from -6 to 6
- w_query: bfloat16 [1024, 1024], replicated, may hold values from -0.1875 to 0.1875
- w_key: bfloat16 [1024, 1024], replicated, may hold values from -0.1875 to 0.1875
- w_value: bfloat16 [1024, 1024], replicated, may hold values from -0.1875 to 0.1875
- w_out: bfloat16 [1024, 4096], P(None, 'patch'), may hold values from -0.1875 to 0.1875
Outputs:
- d_bytes: bfloat16 [65536, 1024], P('seq', 'patch')
- d_qkv: float32 [3, 1024, 1024], P(None, 'patch')
- d_wout: float32 [1024, 4096], P(None, 'patch')
- patch_rows: bfloat16 [8192, 1024], P(('seq', 'patch'))
Inputs may be any that keep to these rules, and one draw needn't show every extreme that they name: `patch_len`: each row sums to 4096. `owner`: each row holds every number of 0 to 511 once.
All inputs are finite; a program needn't handle non-finite values.
Results may differ from a plain program's by a relative error of at most 0.013.
The roundings to bfloat16 on the way count: a program that leaves them out, or rounds other values in their place, can miss the bound.
Values may be sent and summed in bfloat16 or wider, within the bound.
No kernel may reach another device: no remote copies, remote signals or barrier semaphores. Data moves between devices by JAX's collectives and lax.ppermute only.
A program may use at most 192 MiB of HBM per device.

v0:
```python
import jax
import jax.numpy as jnp
from jax import lax
from jax.experimental import pallas as pl
from jax.experimental.pallas import tpu as pltpu
from jax.sharding import PartitionSpec as P

HEADS = 16
MAXP = 16
LANES = 128
TILE = 256
UNROLL = 4
F32, BF16, I16, I32 = jnp.float32, jnp.bfloat16, jnp.int16, jnp.int32
NT = (((1,), (1,)), ((), ()))


def params(mebibytes):
    return pltpu.CompilerParams(vmem_limit_bytes=mebibytes * 1024 * 1024)


def cost(flops, moved):
    return pl.CostEstimate(flops=flops, bytes_accessed=moved, transcendentals=0)


def whole(shape):
    return pl.BlockSpec(shape, lambda *_: (0,) * len(shape))


def smem():
    return pl.BlockSpec(memory_space=pltpu.SMEM)


def dot(a, b):
    return jnp.dot(a, b, preferred_element_type=F32)


def dot_nt(a, b):
    return lax.dot_general(a, b, NT, preferred_element_type=F32)


def coded(value):
    peak = jnp.max(jnp.abs(value), axis=0, keepdims=True)
    power = jnp.ceil(jnp.log2(jnp.maximum(peak, 1e-30)))
    return jnp.round(value * (32767.0 * jnp.exp2(-power))), power


def to_i16(value):
    return value.astype(I32).astype(I16)


def from_i16(value):
    return value.astype(I32).astype(F32)


def unit(power):
    return jnp.exp2(from_i16(power)) * (1.0 / 32767.0)


def padded_rows(row_list, count):
    width = row_list[0].shape[1]
    at = lax.broadcasted_iota(I32, (count, width), 0)
    out = jnp.zeros((count, width), F32)
    for i, row in enumerate(row_list):
        out = jnp.where(at == i, jnp.broadcast_to(row, (count, width)), out)
    return out


def window(bounds, blocks, base):
    block = jnp.int32(0)
    for at in range(1, blocks - 1):
        block = block + (bounds[at] <= base).astype(I32)
    return block


def patch_major(start_ref, end_ref, first, count, base, width):
    rows = pl.ds(pl.multiple_of(first, LANES), count)
    start, end = start_ref[rows, :], end_ref[rows, :]
    parts = []
    for at in range(0, width, LANES):
        byte = base + at + lax.broadcasted_iota(I32, (count, LANES), 1)
        parts.append(jnp.where((byte >= start) & (byte < end), 1.0, 0.0).astype(BF16))
    return parts[0] if len(parts) == 1 else jnp.concatenate(parts, axis=1)


def byte_major(row_ref, first, count, base, width):
    lanes = pl.ds(pl.multiple_of(first, LANES), count)
    byte = base + lax.broadcasted_iota(I32, (width, count), 0)
    inside = (byte >= row_ref[0:1, lanes]) & (byte < row_ref[8:9, lanes])
    return jnp.where(inside, 1.0, 0.0).astype(BF16)


def over_tiles(bounds, blocks, s_dev, rim, body):
    def loop(width, unroll):
        def go(i, carry):
            for at in range(unroll):
                body(pl.multiple_of((i * unroll + at) * width, width), width)
            return carry

        lax.fori_loop(0, s_dev // (unroll * width), go, 0)

    @pl.when(bounds[blocks + 1] == 0)
    def _():
        loop(TILE, UNROLL)

    @pl.when(bounds[blocks + 1] > 0)
    def _():
        loop(LANES, 1)

    body(s_dev, rim)


def fill_rim(rim_ref, rim_rows):
    rim_rows[...] = jnp.zeros_like(rim_rows)
    rim_rows[:rim_ref.shape[0], :] = rim_ref[...]


def columns_of(row_ref, start_ref, end_ref):
    patches = row_ref.shape[1]
    start_ref[...] = jnp.broadcast_to(row_ref[0:1, :], (LANES, patches)).T
    end_ref[...] = jnp.broadcast_to(row_ref[8:9, :], (LANES, patches)).T


def send_copies(source, target, sems):
    copies = [pltpu.make_async_copy(source, target.at[i], sems.at[i]) for i in range(target.shape[0])]
    for copy in copies:
        copy.start()
    return copies


def over_segment(value, place, left, op):
    size = value.shape[1]
    before, after = value, value
    for step in (1, 2, 4, 8):
        before = jnp.where(place >= step, op(before, pltpu.roll(before, step, 1)), before)
        after = jnp.where(left >= step, op(after, pltpu.roll(after, size - step, 1)), after)
    return before, after


def head_rows(rows, dim):
    count, width = rows.shape
    return jnp.concatenate(
        [jnp.broadcast_to(rows[i:i + 1], (dim, width)) for i in range(count)], axis=0
    )


def split2(value):
    high = value.astype(BF16)
    return jnp.concatenate([high, (value - high.astype(F32)).astype(BF16)], axis=0)


def att_grad_kernel(w_ref, cot_ref, out_ref, cot_t):
    groups = out_ref.shape[0]
    own = w_ref.shape[0] // groups
    cot_t[...] = cot_ref[...].astype(F32).T.astype(BF16)
    for group in range(groups):
        codes, power = coded(dot(w_ref[group * own:(group + 1) * own, :], cot_t[...]))
        out_ref[group, :own, :] = to_i16(codes)
        out_ref[group, own:, :] = to_i16(jnp.broadcast_to(power, (16, power.shape[1])))


def att_grad(w_out, cot, groups):
    width, cols = w_out.shape
    rows = cot.shape[0]
    own = width // groups
    return pl.pallas_call(
        att_grad_kernel,
        in_specs=[pl.BlockSpec(memory_space=pltpu.VMEM)] * 2,
        out_specs=pl.BlockSpec(memory_space=pltpu.VMEM),
        out_shape=jax.ShapeDtypeStruct((groups, own + 16, rows), I16),
        scratch_shapes=[pltpu.VMEM((cols, rows), BF16)],
        compiler_params=params(56),
        cost_estimate=cost(2 * width * cols * rows, 4 << 20),
        name="att_grad",
    )(w_out, cot)


def forward_kernel(
    member, offset, len_ref, x_hbm, wq_hbm, rim_ref, wk_ref, wv_ref,
    kv_hbm, pooled_hbm, queries_hbm, att_ref, query_ref, probs_ref, geo_ref, row_ref, bounds,
    rim_rows, x_ref, wq_ref, queries_ref, kv_ref, pooled_ref, w_kv, acc, lhs, start_ref, end_ref, inv_col, att_acc,
    x_sems, out_sems,
):
    rim = rim_rows.shape[0]
    patches = len_ref.shape[1]
    blocks = patches // LANES
    own = wk_ref.shape[1]
    dim = 64
    heads = own // dim
    s_dev = x_hbm.shape[0]
    chunks = x_sems.shape[0]
    chunk = s_dev // chunks
    loads = []
    for i in range(chunks):
        at = slice(i * chunk, (i + 1) * chunk)
        loads.append(pltpu.make_async_copy(x_hbm.at[at, :], x_ref.at[at, :], x_sems.at[i]))
        loads[-1].start()
    wq_copy = pltpu.make_async_copy(wq_hbm, wq_ref, out_sems.at[2])
    wq_copy.start()

    length = len_ref[...].astype(F32)
    before = lax.broadcasted_iota(I32, (patches, patches), 0)
    after = lax.broadcasted_iota(I32, (patches, patches), 1)
    off = offset[0].astype(F32)
    eight = jnp.broadcast_to(length, (8, patches))
    upper = jnp.where(before < after, 1.0, 0.0).astype(BF16)
    start_row = (dot(eight.astype(BF16), upper) + off).astype(I32)
    row_ref[:8, :] = start_row
    row_ref[8:, :] = start_row + eight.astype(I32)
    columns_of(row_ref, start_ref, end_ref)
    inv_col[...] = 1.0 / jnp.broadcast_to(length, (LANES, patches)).T
    at = lax.broadcasted_iota(I32, (16, patches), 0)
    both = jnp.concatenate([start_row, start_row], axis=0)
    geo = jnp.where(at == 0, both >> 6, jnp.where(at == 1, both & 63, 0)).astype(F32)
    geo = jnp.where(at == 2, jnp.broadcast_to(length, (16, patches)), geo)
    lhs[own:own + 16, :] = geo.astype(BF16)
    lane = lax.broadcasted_iota(I32, (1, patches), 1)
    for block in range(blocks + 1):
        total = jnp.sum(jnp.where(lane < block * LANES, length, 0.0))
        bounds[block] = (total + off).astype(I32)

    def crowded(i, found):
        base = i * TILE
        third = window(bounds, blocks, base) + 2
        return found | ((third < blocks) & (bounds[third] < base + TILE)).astype(I32)

    bounds[blocks + 1] = lax.fori_loop(0, s_dev // TILE, crowded, jnp.int32(0))
    w_kv[:, :own] = wk_ref[...]
    w_kv[:, own:] = wv_ref[...]
    acc[...] = jnp.zeros_like(acc)

    def project(rows, base, width):
        kv_ref[:, pl.ds(base, width)] = dot(rows, w_kv[...]).T.astype(BF16)
        first = pl.multiple_of(window(bounds, blocks, base) * LANES, LANES)
        at = pl.ds(first, 2 * LANES)
        acc[at, :] += dot(patch_major(start_ref, end_ref, first, 2 * LANES, base, width), rows)

    for i in range(chunks):
        loads[i].wait()
        for at in range(i * chunk, (i + 1) * chunk, TILE):
            project(x_ref[at:at + TILE, :], at, TILE)
    fill_rim(rim_ref, rim_rows)
    project(rim_rows[...], s_dev, rim)

    @pl.when(bounds[blocks + 1] > 0)
    def _():
        def rest(i, carry):
            base = pl.multiple_of(i * TILE, TILE)
            third = window(bounds, blocks, base) + 2

            @pl.when((third < blocks) & (bounds[third] < base + TILE))
            def _():
                first = pl.multiple_of(third * LANES, LANES)
                acc[pl.ds(first, LANES), :] += dot(
                    patch_major(start_ref, end_ref, first, LANES, base, TILE), x_ref[pl.ds(base, TILE), :]
                )

            return carry

        lax.fori_loop(0, s_dev // TILE, rest, 0)

    kv_copy = pltpu.make_async_copy(kv_ref, kv_hbm, out_sems.at[0])
    kv_copy.start()
    pooled = (acc[...] * inv_col[:, :1]).astype(BF16)
    pooled_ref[...] = pooled
    pooled_copy = pltpu.make_async_copy(pooled_ref, pooled_hbm, out_sems.at[1])
    pooled_copy.start()
    wq_copy.wait()
    queries_ref[...] = dot(pooled, wq_ref[...]).T.astype(BF16)
    queries_copy = pltpu.make_async_copy(queries_ref, queries_hbm, out_sems.at[3])
    queries_copy.start()
    query = queries_ref[pl.ds(pl.multiple_of(member[0] * own, own), own), :]
    lhs[:own, :] = query
    query_ref[...] = query

    def score(base, width):
        first = pl.multiple_of(window(bounds, blocks, base) * LANES, LANES)
        exp = dot(
            lhs[:, pl.ds(first, 2 * LANES)],
            patch_major(start_ref, end_ref, first, 2 * LANES, base, width),
        )
        at = pl.ds(base, width)
        product = exp[:own] * kv_ref[:own, at].astype(F32)
        rows = [jnp.sum(product[h * dim:(h + 1) * dim], axis=0, keepdims=True) for h in range(heads)]
        probs_ref[:, at] = padded_rows(rows, 8) * (dim ** -0.5)
        geo = exp[own:own + 8]
        byte = (base + lax.broadcasted_iota(I32, (1, width), 1)).astype(F32)
        place = byte - (64.0 * geo[0:1] + geo[1:2])
        geo_ref[:, at] = padded_rows([place, geo[2:3] - 1.0 - place], 8)

    over_tiles(bounds, blocks, s_dev, rim, score)
    place, left = geo_ref[0:1, :], geo_ref[1:2, :]
    scores = probs_ref[...]
    before, after = over_segment(scores, place, left, jnp.maximum)
    expo = jnp.exp(scores - jnp.maximum(before, after))
    before, after = over_segment(expo, place, left, jnp.add)
    probs_ref[...] = jnp.where(left >= 0.0, expo / (before + (after - expo)), 0.0)
    att_acc[...] = jnp.zeros_like(att_acc)

    def attend(base, width):
        at = pl.ds(base, width)
        probs_b = probs_ref[:, at].astype(BF16).astype(F32)[:heads]
        both = split2(head_rows(probs_b, dim) * kv_ref[own:, at].astype(F32))
        first = pl.multiple_of(window(bounds, blocks, base) * LANES, LANES)
        att_acc[:, pl.ds(first, 2 * LANES)] += dot(
            both, byte_major(row_ref, first, 2 * LANES, base, width)
        )

    over_tiles(bounds, blocks, s_dev, rim, attend)
    att_ref[...] = (att_acc[:own, :] + att_acc[own:, :]).astype(BF16)
    for copy in (kv_copy, pooled_copy, queries_copy):
        copy.wait()


def hbm():
    return pl.BlockSpec(memory_space=pltpu.HBM)


def near():
    return pl.BlockSpec(memory_space=pl.ANY)


def forward(member, offset, lengths, x, rim, w_key, w_value, w_query, groups):
    s_dev, width = x.shape
    patches = lengths.shape[1]
    own = width // groups
    total = s_dev + LANES
    col = pl.BlockSpec((width, own), lambda i, member, offset: (0, member[0]))
    shape = jax.ShapeDtypeStruct
    small = [
        shape((own, patches), BF16), shape((own, patches), BF16), shape((8, total), F32), shape((8, total), F32), shape((16, patches), I32),
    ]
    return pl.pallas_call(
        forward_kernel,
        grid_spec=pltpu.PrefetchScalarGridSpec(
            num_scalar_prefetch=2,
            grid=(1,),
            in_specs=[whole(lengths.shape), hbm(), hbm(), whole(rim.shape), col, col],
            out_specs=[hbm()] * 3 + [whole(s.shape) for s in small] + [smem()],
            scratch_shapes=[
                pltpu.VMEM((LANES, width), BF16),
                pltpu.VMEM((s_dev, width), BF16),
                pltpu.VMEM((width, width), BF16),
                pltpu.VMEM((width, patches), BF16),
                pltpu.VMEM((2 * own, total), BF16),
                pltpu.VMEM((patches, width), BF16),
                pltpu.VMEM((width, 2 * own), BF16),
                pltpu.VMEM((patches, width), F32),
                pltpu.VMEM((own + 16, patches), BF16),
                pltpu.VMEM((patches, LANES), I32),
                pltpu.VMEM((patches, LANES), I32),
                pltpu.VMEM((patches, LANES), F32),
                pltpu.VMEM((2 * own, patches), F32),
                pltpu.SemaphoreType.DMA((8,)),
                pltpu.SemaphoreType.DMA((4,)),
            ],
        ),
        out_shape=[shape((2 * own, total), BF16), shape((patches, width), BF16), shape((width, patches), BF16)]
        + small + [shape((8,), I32)],
        compiler_params=params(56),
        cost_estimate=cost(8 << 30, 12 << 20),
        name="forward",
    )(member, offset, lengths, x, w_query, rim, w_key, w_value)


def att_sum_kernel(got_ref, out_ref):
    own = out_ref.shape[0]
    total = jnp.zeros(out_ref.shape, F32)
    for source in range(got_ref.shape[0]):
        total = total + from_i16(got_ref[source, :own, :]) * unit(got_ref[source, own:, :])[0:1]
    out_ref[...] = total.astype(BF16)


def att_sum(got):
    groups, rows, patches = got.shape
    vmem = pl.BlockSpec(memory_space=pltpu.VMEM)
    return pl.pallas_call(
        att_sum_kernel,
        in_specs=[vmem],
        out_specs=vmem,
        out_shape=jax.ShapeDtypeStruct((rows - 16, patches), BF16),
        compiler_params=params(8),
        cost_estimate=cost(1 << 20, 2 << 20),
        name="att_sum",
    )(got)


def backward_kernel(
    bounds, x_hbm, kv_hbm, pooled_hbm, rim_ref, d_att_ref, query_ref, probs_ref, geo_ref, row_ref,
    grad_ref, factor_out,
    rim_rows, x_ref, kv_ref, pooled_ref, factor_ref, start_ref, end_ref, d_kv, lhs, d_probs, d_scores, dq_acc, acc,
    x_sems, in_sems,
):
    rim = rim_rows.shape[0]
    s_dev = x_hbm.shape[0]
    own, patches = query_ref.shape
    blocks = patches // LANES
    dim = 64
    heads = own // dim
    kv_copy = pltpu.make_async_copy(kv_hbm, kv_ref, in_sems.at[0])
    kv_copy.start()
    chunks = x_sems.shape[0]
    chunk = s_dev // chunks
    loads = []
    for i in range(chunks):
        at = slice(i * chunk, (i + 1) * chunk)
        loads.append(pltpu.make_async_copy(x_hbm.at[at, :], x_ref.at[at, :], x_sems.at[i]))
    pooled_copy = pltpu.make_async_copy(pooled_hbm, pooled_ref, in_sems.at[1])

    columns_of(row_ref, start_ref, end_ref)
    lhs[:own, :] = d_att_ref[...]
    lhs[own:, :] = query_ref[...]
    factor_ref[:own, :] = d_att_ref[...]
    kv_copy.wait()
    for copy in loads + [pooled_copy]:
        copy.start()

    def first_pass(base, width):
        first = pl.multiple_of(window(bounds, blocks, base) * LANES, LANES)
        exp = dot(
            lhs[:, pl.ds(first, 2 * LANES)],
            patch_major(start_ref, end_ref, first, 2 * LANES, base, width),
        )
        d_out = exp[:own]
        at = pl.ds(base, width)
        product = d_out * kv_ref[own:, at].astype(F32)
        rows = [jnp.sum(product[h * dim:(h + 1) * dim], axis=0, keepdims=True) for h in range(heads)]
        d_probs[:, at] = padded_rows(rows, 8)
        probs_b = probs_ref[:, at].astype(BF16).astype(F32)[:heads]
        d_kv[own:, at] = (head_rows(probs_b, dim) * d_out).astype(BF16)
        d_kv[:own, at] = exp[own:].astype(BF16)

    over_tiles(bounds, blocks, s_dev, rim, first_pass)
    place, left = geo_ref[0:1, :], geo_ref[1:2, :]
    probs = probs_ref[...]
    weighted = probs * d_probs[...]
    before, after = over_segment(weighted, place, left, jnp.add)
    inner = before + (after - weighted)
    slope = jnp.where(left >= 0.0, probs * (d_probs[...] - inner) * (dim ** -0.5), 0.0)
    d_scores[...] = slope.astype(BF16).astype(F32)
    dq_acc[...] = jnp.zeros_like(dq_acc)

    def second_pass(base, width):
        at = pl.ds(base, width)
        wide = head_rows(d_scores[:, at][:heads], dim)
        d_kv[:own, at] = (wide * d_kv[:own, at].astype(F32)).astype(BF16)
        both = split2(wide * kv_ref[:own, at].astype(F32))
        first = pl.multiple_of(window(bounds, blocks, base) * LANES, LANES)
        dq_acc[:, pl.ds(first, 2 * LANES)] += dot(
            both, byte_major(row_ref, first, 2 * LANES, base, width)
        )

    over_tiles(bounds, blocks, s_dev, rim, second_pass)
    factor_ref[own:2 * own, :] = (dq_acc[:own, :] + dq_acc[own:, :]).astype(BF16)
    probs_b = probs.astype(BF16).astype(F32)
    rows = padded_rows(
        [d_scores[h:h + 1, :] for h in range(heads)] + [probs_b[h:h + 1, :] for h in range(heads)], 8
    )
    groups = [rows[:, at:at + patches] for at in range(0, s_dev, patches)]
    groups.append(jnp.concatenate([rows[:, s_dev:], jnp.zeros((8, patches - rim), F32)], axis=1))
    groups += [jnp.zeros((8, patches), F32)] * ((factor_ref.shape[0] - 2 * own) // 4 - len(groups))
    upper = lax.broadcasted_iota(I32, (8, patches), 0) < 4
    stack = [
        jnp.where(upper, groups[i], pltpu.roll(groups[i + 1], 4, 0)) for i in range(0, len(groups), 2)
    ]
    factor_ref[2 * own:, :] = jnp.concatenate(stack, axis=0).astype(BF16)
    factor_out[...] = factor_ref[...]

    fill_rim(rim_ref, rim_rows)
    acc[...] = dot(d_kv[:, s_dev:], rim_rows[...])
    for i in range(chunks):
        loads[i].wait()
    acc[...] += dot(d_kv[:, :s_dev], x_ref[...])
    pooled_copy.wait()
    grad_q = dot(factor_ref[own:2 * own, :], pooled_ref[...])
    powers = []
    parts = grad_ref.shape[0]
    for k, grad in enumerate((grad_q, acc[:own, :], acc[own:, :])):
        codes, power = coded(grad.T)
        powers.append(power)
        rows = codes.shape[0] // parts
        spread = codes.reshape(rows // 8, parts, 8, own)
        for part in range(parts):
            grad_ref[part, k * rows:(k + 1) * rows, :] = to_i16(spread[:, part].reshape(rows, own))
    tail = to_i16(padded_rows(powers, 16))
    for part in range(parts):
        grad_ref[part, 3 * rows:, :] = tail


def backward(bounds, x, kv, pooled, rim, d_att, query, probs, geo, row, parts):
    s_dev, width = x.shape
    own, patches = query.shape
    total = kv.shape[1]
    extra = -(-4 * (s_dev // patches + 1) // 16) * 16
    rows = width // parts
    vmem = pl.BlockSpec(memory_space=pltpu.VMEM)
    return pl.pallas_call(
        backward_kernel,
        in_specs=[smem()] + [hbm()] * 3 + [vmem] * 6,
        out_specs=[vmem, vmem],
        out_shape=[
            jax.ShapeDtypeStruct((parts, 3 * rows + 16, own), I16),
            jax.ShapeDtypeStruct((2 * own + extra, patches), BF16),
        ],
        scratch_shapes=[
            pltpu.VMEM((LANES, width), BF16),
            pltpu.VMEM((s_dev, width), BF16),
            pltpu.VMEM((2 * own, total), BF16),
            pltpu.VMEM((patches, width), BF16),
            pltpu.VMEM((2 * own + extra, patches), BF16),
            pltpu.VMEM((patches, LANES), I32),
            pltpu.VMEM((patches, LANES), I32),
            pltpu.VMEM((2 * own, total), BF16),
            pltpu.VMEM((2 * own, patches), BF16),
            pltpu.VMEM((8, total), F32),
            pltpu.VMEM((8, total), F32),
            pltpu.VMEM((2 * own, patches), F32),
            pltpu.VMEM((2 * own, width), F32),
            pltpu.SemaphoreType.DMA((4,)),
            pltpu.SemaphoreType.DMA((2,)),
        ],
        compiler_params=params(56),
        cost_estimate=cost(6 << 30, 16 << 20),
        name="backward",
    )(bounds, x, kv, pooled, rim, d_att, query, probs, geo, row)


def out_grad_kernel(member, mine_ref, other_ref, cot_ref, owner_ref, out_ref, rows_ref, att_ref):
    chips, own, patches = mine_ref.shape
    chip, core = member[0] // 2, member[0] % 2
    for ref, ref_core in ((mine_ref, core), (other_ref, 1 - core)):
        for back in range(chips):
            group = 2 * lax.rem(chip + chips - back, chips) + ref_core
            att_ref[pl.ds(pl.multiple_of(group * own, own), own), :] = ref[back]
    att = att_ref[...]
    codes, power = coded(dot(att, cot_ref[...]))
    parts = out_ref.shape[0]
    rows = codes.shape[0] // parts
    slabs = codes.shape[1] // LANES
    tail = to_i16(padded_rows([power[:, at * LANES:(at + 1) * LANES] for at in range(slabs)], 16))
    for part in range(parts):
        for at in range(slabs):
            block = codes[part * rows:(part + 1) * rows, at * LANES:(at + 1) * LANES]
            out_ref[part, at * rows:(at + 1) * rows, :] = to_i16(block)
        out_ref[part, slabs * rows:, :] = tail
    count = rows_ref.shape[0]
    order = jnp.broadcast_to(owner_ref[...], (8, patches))
    order = pltpu.roll(order, lax.rem(patches - member[0] * count, patches), 1)[0:1, :LANES]
    pick = jnp.where(lax.broadcasted_iota(I32, (patches, LANES), 0) == order, 1.0, 0.0).astype(BF16)
    rows_ref[...] = dot(att, pick).T[:count].astype(BF16)


def out_grad(member, mine, other, cot, owner, parts):
    chips, own, patches = mine.shape
    groups = 2 * chips
    width, cols = groups * own, cot.shape[1]
    rows = cols // LANES * (width // parts) + 16
    count = patches // groups
    return pl.pallas_call(
        out_grad_kernel,
        in_specs=[smem()] + [pl.BlockSpec(memory_space=pltpu.VMEM)] * 4,
        out_specs=[pl.BlockSpec(memory_space=pltpu.VMEM)] * 2,
        scratch_shapes=[pltpu.VMEM((width, patches), BF16)],
        out_shape=[
            jax.ShapeDtypeStruct((parts, rows, LANES), I16),
            jax.ShapeDtypeStruct((count, width), BF16),
        ],
        compiler_params=params(16),
        cost_estimate=cost(2 * width * cols * patches, 4 << 20),
        name="out_grad",
    )(member, mine, other, cot, owner)


def decoded(got_ref, first, count, power_row):
    rows = got_ref.shape[1]
    total = jnp.zeros((count, got_ref.shape[2]), F32)
    for source in range(got_ref.shape[0]):
        scale = unit(got_ref[source, rows - 16:, :])[power_row:power_row + 1]
        total = total + from_i16(got_ref[source, first:first + count, :]) * scale
    return total


def qkv_sum_kernel(member, got_ref, *refs):
    outs, blocks = refs[:-1], refs[-1]
    chips = len(outs)
    count = (got_ref.shape[1] - 16) // 3
    totals = [decoded(got_ref, k * count, count, k) for k in range(3)]
    for group in range(2 * chips):
        rows = [total[group * 8:(group + 1) * 8] for total in totals]
        rows = jnp.concatenate(rows + [jnp.zeros_like(rows[0])], axis=0)
        blocks[group // 2, group % 2 * 32:group % 2 * 32 + 32, :] = rows
    for at, out in enumerate(outs):
        out[...] = blocks[(member[0] // 2) ^ at].astype(BF16)


def qkv_sum(member, got, chips):
    vmem = pl.BlockSpec(memory_space=pltpu.VMEM)
    return pl.pallas_call(
        qkv_sum_kernel,
        in_specs=[smem(), vmem],
        out_specs=[vmem] * chips,
        out_shape=[jax.ShapeDtypeStruct((64, LANES), BF16)] * chips,
        scratch_shapes=[pltpu.VMEM((chips, 64, LANES), F32)],
        compiler_params=params(8),
        cost_estimate=cost(1 << 20, 2 << 20),
        name="qkv_sum",
    )(member, got)


def stack_kernel(*refs):
    out = refs[-1]
    for at, block in enumerate(refs[:-1]):
        out[at] = block[...]


def stack(blocks):
    vmem = pl.BlockSpec(memory_space=pltpu.VMEM)
    return pl.pallas_call(
        stack_kernel,
        in_specs=[vmem] * len(blocks),
        out_specs=vmem,
        out_shape=jax.ShapeDtypeStruct((len(blocks),) + blocks[0].shape, BF16),
        compiler_params=params(8),
        cost_estimate=cost(1 << 16, 1 << 20),
        name="stack",
    )(*blocks)


def relay_kernel(member, *refs):
    chips = (len(refs) - 5) // 2
    blocks, columns = refs[:chips], refs[chips:2 * chips]
    keep_ref, send_ref, mine_any, stage, sems = refs[2 * chips:]
    moves = [pltpu.make_async_copy(column, stage.at[i], sems.at[i]) for i, column in enumerate(columns)]
    for copy in moves:
        copy.start()
    core = member[0] % 2
    for at, block in enumerate(blocks):
        keep_ref[at * 32:(at + 1) * 32, :] = block[pl.ds(pl.multiple_of(core * 32, 32), 32), :]
        send_ref[at * 32:(at + 1) * 32, :] = block[pl.ds(pl.multiple_of((1 - core) * 32, 32), 32), :]
    sends = [pltpu.make_async_copy(stage.at[i], mine_any.at[i], sems.at[chips + i]) for i in range(chips)]
    for copy, send in zip(moves, sends):
        copy.wait()
        send.start()
    for send in sends:
        send.wait()


def relay(member, blocks, columns):
    vmem = pl.BlockSpec(memory_space=pltpu.VMEM)
    chips = len(blocks)
    return pl.pallas_call(
        relay_kernel,
        in_specs=[smem()] + [vmem] * chips + [near()] * chips,
        out_specs=[vmem, vmem, near()],
        out_shape=[
            jax.ShapeDtypeStruct((32 * chips, LANES), BF16),
            jax.ShapeDtypeStruct((32 * chips, LANES), BF16),
            jax.ShapeDtypeStruct((chips,) + columns[0].shape, BF16),
        ],
        scratch_shapes=[
            pltpu.VMEM((chips,) + columns[0].shape, BF16), pltpu.SemaphoreType.DMA((2 * chips,)),
        ],
        compiler_params=params(8),
        cost_estimate=cost(1 << 16, 3 << 20),
        name="relay",
    )(member, *blocks, *columns)


def pack_kernel(got_ref, keep_ref, other_ref, out_hbm, pack, sems):
    chips = keep_ref.shape[0] // 32
    rows = []
    for ref in (keep_ref, other_ref):
        values = ref[...].astype(F32)
        rows += [values[at * 32:at * 32 + 24] for at in range(chips)]
    first = 24 * len(rows)
    pack[:first, :] = jnp.concatenate(rows, axis=0).astype(BF16)
    count = (pack.shape[0] - first) // 4
    for slab in range(4):
        total = decoded(got_ref, slab * count, count, slab)
        pack[first + slab * count:first + (slab + 1) * count, :] = total.astype(BF16)
    for copy in send_copies(pack, out_hbm, sems):
        copy.wait()


def pack_sums(got, keep, other, parts):
    vmem = pl.BlockSpec(memory_space=pltpu.VMEM)
    rows = 24 * (keep.shape[0] // 16) + got.shape[1] - 16
    return pl.pallas_call(
        pack_kernel,
        in_specs=[vmem] * 3,
        out_specs=hbm(),
        out_shape=jax.ShapeDtypeStruct((parts, rows, LANES), BF16),
        scratch_shapes=[pltpu.VMEM((rows, LANES), BF16), pltpu.SemaphoreType.DMA((parts,))],
        compiler_params=params(60),
        cost_estimate=cost(1 << 20, 3 << 20),
        name="pack_sums",
    )(got, keep, other)


def unpack_kernel(member, got_ref, qkv_hbm, wout_hbm, qkv_ref, wout_ref, out_sems):
    parts, rows, lanes = got_ref.shape
    steps = out_sems.shape[0] // 2
    per = parts // steps
    groups = qkv_ref.shape[2] // lanes
    first = 24 * groups
    count = wout_ref.shape[0] // parts
    stores = []
    for step in range(steps):
        for part in range(step * per, (step + 1) * per):
            for slab in range(wout_ref.shape[1] // lanes):
                block = got_ref[part, first + slab * count:first + (slab + 1) * count, :]
                wout_ref[part * count:(part + 1) * count, slab * lanes:(slab + 1) * lanes] = block.astype(F32)
            values = got_ref[part, :first, :].astype(F32)
            for at in range(groups):
                source = member[0] ^ (2 * (at % (groups // 2)) + at // (groups // 2))
                lane = pl.ds(pl.multiple_of(source * lanes, lanes), lanes)
                for k in range(3):
                    top = at * 24 + k * 8
                    qkv_ref[k, part * 8:(part + 1) * 8, lane] = values[top:top + 8]
        at = slice(step * per * count, (step + 1) * per * count)
        stores.append(pltpu.make_async_copy(wout_ref.at[at, :], wout_hbm.at[at, :], out_sems.at[2 * step]))
        stores[-1].start()
        at = slice(step * per * 8, (step + 1) * per * 8)
        stores.append(pltpu.make_async_copy(qkv_ref.at[:, at, :], qkv_hbm.at[:, at, :], out_sems.at[2 * step + 1]))
        stores[-1].start()
    for copy in stores:
        copy.wait()


def unpack_sums(member, got, width, cols, groups):
    steps = 4
    qkv = ((3, width // groups, width), F32)
    wout = ((width, cols), F32)
    return pl.pallas_call(
        unpack_kernel,
        in_specs=[smem(), pl.BlockSpec(memory_space=pltpu.VMEM)],
        out_specs=[hbm(), hbm()],
        out_shape=[jax.ShapeDtypeStruct(*qkv), jax.ShapeDtypeStruct(*wout)],
        scratch_shapes=[
            pltpu.VMEM(*qkv), pltpu.VMEM(*wout), pltpu.SemaphoreType.DMA((2 * steps,)),
        ],
        compiler_params=params(12),
        cost_estimate=cost(1 << 20, 6 << 20),
        name="unpack_sums",
    )(member, got)


def bytes_kernel(
    member, bounds, mine_hbm, other_hbm, query_hbm, wk_hbm, wv_hbm, wq_hbm, row_ref,
    out_ref, head_ref, tail_ref,
    lhs, d_query, tables, shares, d_kv, w_own, wq_own, start_ref, end_ref, sems,
):
    chips, rows, patches = mine_hbm.shape
    groups = 2 * chips
    own, width = wq_own.shape
    dim = 64
    heads = own // dim
    blocks = patches // LANES
    total = shares.shape[2]
    s_dev = out_ref.shape[0]
    rim = total - s_dev
    chip, core = member[0] // 2, member[0] % 2
    own_rows = pl.ds(pl.multiple_of(member[0] * own, own), own)
    moves = []

    def move(source, target):
        moves.append(pltpu.make_async_copy(source, target, sems.at[len(moves)]))
        moves[-1].start()

    places = []
    for ref, ref_core in ((mine_hbm, core), (other_hbm, 1 - core)):
        for back in range(chips):
            group = 2 * lax.rem(chip + chips - back, chips) + ref_core
            at = pl.multiple_of(group * own, own)
            places.append(group)
            move(ref.at[back, 2 * own:, :], tables.at[len(places) - 1])
            move(ref.at[back, own:2 * own, :], d_query.at[pl.ds(at, own), :])
            move(ref.at[back, :own, :], lhs.at[pl.ds(width + at, own), :])
    move(wq_hbm.at[own_rows, :], wq_own)
    move(query_hbm, lhs.at[:width, :])
    move(wk_hbm.at[own_rows, :], w_own.at[:, :width])
    move(wv_hbm.at[own_rows, :], w_own.at[:, width:])
    columns_of(row_ref, start_ref, end_ref)
    for copy in moves:
        copy.wait()
    for slot, group in enumerate(places):
        table = tables[slot].astype(F32)
        for at in range(s_dev // patches + 1):
            part = table[8 * (at // 2):8 * (at // 2) + 8]
            part = pltpu.roll(part, 4, 0) if at % 2 else part
            if at < s_dev // patches:
                shares[group, :, at * patches:(at + 1) * patches] = part
            else:
                shares[group, :, s_dev:] = part[:, :rim]
    length = (row_ref[8:9, :] - row_ref[0:1, :]).astype(F32)
    lhs[2 * width:, :] = split2(dot(wq_own[...], d_query[...]) * (1.0 / length))

    def tile_grad(base, span, first, count, slot):
        inside = patch_major(start_ref, end_ref, first, count, base, span)
        at = pl.ds(base, span)
        patch = pl.ds(first, count)
        for group in range(groups):
            share = shares[group, :, at]
            for kind in range(2):
                top = kind * width + group * own
                wide = dot(lhs[top:top + own, patch], inside)
                part = head_rows(share[kind * heads:(kind + 1) * heads], dim)
                d_kv[slot, top:top + own, :span] = (part * wide).astype(BF16)
        grad = dot(w_own[...], d_kv[slot, :, :span])
        pool = dot(lhs[2 * width:, patch], inside)
        return (grad + (pool[:own] + pool[own:])).T

    def tiles(span, first_of, count):
        def go(i, carry):
            for slot in range(UNROLL):
                base = pl.multiple_of((UNROLL * i + slot) * span, span)
                out_ref[pl.ds(base, span), :] = tile_grad(base, span, first_of(base), count, slot).astype(BF16)
            return carry

        lax.fori_loop(0, s_dev // (UNROLL * span), go, 0)

    def first_of(base):
        return pl.multiple_of(window(bounds, blocks, base) * LANES, LANES)

    @pl.when(bounds[blocks + 1] > 0)
    def _():
        tiles(LANES, first_of, 2 * LANES)

    @pl.when(bounds[blocks + 1] == 0)
    def _():
        tiles(TILE, first_of, 2 * LANES)

    head_ref[...] = tile_grad(0, LANES, 0, 2 * LANES, 0)[:16]
    tail_ref[...] = tile_grad(s_dev, rim, patches - 2 * LANES, 2 * LANES, 1)[:16]


def byte_grads(member, bounds, mine_factors, other_factors, query, w_query, w_key, w_value, row, s_dev):
    chips, rows, patches = mine_factors.shape
    groups = 2 * chips
    width = w_query.shape[0]
    own = width // groups
    rim = LANES
    return pl.pallas_call(
        bytes_kernel,
        in_specs=[smem(), smem(), near(), near()] + [hbm()] * 4 + [pl.BlockSpec(memory_space=pltpu.VMEM)],
        out_specs=[pl.BlockSpec(memory_space=pltpu.VMEM)] * 3,
        scratch_shapes=[
            pltpu.VMEM((2 * width + 2 * own, patches), BF16),
            pltpu.VMEM((width, patches), BF16),
            pltpu.VMEM((groups, rows - 2 * own, patches), BF16),
            pltpu.VMEM((groups, 8, s_dev + rim), F32),
            pltpu.VMEM((UNROLL, 2 * width, TILE), BF16),
            pltpu.VMEM((own, 2 * width), BF16),
            pltpu.VMEM((own, width), BF16),
            pltpu.VMEM((patches, LANES), I32),
            pltpu.VMEM((patches, LANES), I32),
            pltpu.SemaphoreType.DMA((3 * groups + 4,)),
        ],
        out_shape=[
            jax.ShapeDtypeStruct((s_dev, own), BF16),
            jax.ShapeDtypeStruct((16, own), F32),
            jax.ShapeDtypeStruct((16, own), F32),
        ],
        compiler_params=params(52),
        cost_estimate=cost(8 << 30, 8 << 20),
        name="byte_grads",
    )(member, bounds, mine_factors, other_factors, query, w_key, w_value, w_query, row)


def shifted(value, axis, steps):
    count = lax.axis_size(axis)
    first, last = (max(0, -steps), min(count, count - steps))
    return lax.ppermute(value, axis, [(source, source + steps) for source in range(first, last)])


def swap(value, axis):
    return lax.all_to_all(value, axis, split_axis=0, concat_axis=0, tiled=True)


def over_chips(value):
    count = lax.axis_size("patch")
    blocks = [value]
    for step in range(1, count // 2):
        pairs = [(i, (i + 2 * step) % count) for i in range(count)]
        blocks.append(lax.ppermute(value, "patch", pairs))
    return blocks


def other_core(value):
    return lax.ppermute(value, "patch", [(i, i ^ 1) for i in range(lax.axis_size("patch"))])


def after(value, *others):
    return lax.optimization_barrier((value,) + others)[0]


def local(byte_states, patch_len, shard_offset, owner, cotangent, w_query, w_key, w_value, w_out):
    s_dev, width = byte_states.shape
    groups = lax.axis_size("patch")
    parts = lax.axis_size("seq")
    member = lax.axis_index("patch").astype(I32).reshape(1)
    rim = shifted(byte_states[:MAXP], "seq", -1)

    coded_att = after(att_grad(w_out, cotangent, groups), rim)
    got_att = swap(coded_att, "patch")
    kv, pooled, all_query, att, query, probs, geo, row, bounds = forward(
        member, shard_offset, patch_len, byte_states, rim, w_key, w_value, w_query, groups
    )
    att_columns = over_chips(att)
    grads, factor = backward(bounds, byte_states, kv, pooled, rim, att_sum(got_att), query, probs, geo, row, parts)
    got_qkv = swap(after(grads, *att_columns[1:]), "seq")
    mine_att = stack([after(att_columns[0], grads)] + att_columns[1:])
    other_att = other_core(mine_att)
    columns = over_chips(factor)
    coded_out, patch_rows = out_grad(member, mine_att, other_att, cotangent, owner, parts)
    got_out = swap(after(coded_out, got_qkv, columns[1], columns[3]), "seq")
    blocks = [
        block if at == 0 else lax.ppermute(block, "patch", [(i, i ^ (2 * at)) for i in range(groups)])
        for at, block in enumerate(qkv_sum(member, got_qkv, groups // 2))
    ]
    keep, send, mine = relay(member, blocks, columns)
    got_keep = other_core(send)
    other = other_core(mine)
    sums = swap(pack_sums(got_out, keep, got_keep, parts), "seq")
    d_bytes, head, tail = byte_grads(
        member, bounds, mine, other, all_query, w_query, w_key, w_value, row, s_dev
    )
    first = (head + shifted(tail, "seq", 1)).astype(BF16)
    d_bytes = lax.dynamic_update_slice(d_bytes, first, (0, 0))
    d_qkv, d_wout = unpack_sums(member, sums, width, cotangent.shape[1], groups)
    return (d_bytes, d_qkv, d_wout, patch_rows)


def solution(mesh):
    return jax.shard_map(
        local,
        mesh=mesh,
        in_specs=(
            P("seq", None), P("seq", None), P("seq"), P("seq", None), P("seq", "patch"),
            P(), P(), P(), P(None, "patch"),
        ),
        out_specs=(P("seq", "patch"), P(None, "patch", None), P(None, "patch"), P(("seq", "patch"), None)),
        check_vma=False,
    )
```

profile of v0, /device:TPU:0, one launch (start us, length us, event | category | flops | bytes accessed | tf_op | source)
XLA Modules:
  0.0 133.2 jit_solution(364781158542993630)
XLA Ops:
  0.6 0.8 slice.3
  1.4 1.3 collective-permute-start
  2.7 3.3 %att_grad.1 = s16[8,144,512]{2,1,0:T(8,128)(2,1)} custom-call(bf16[1024,512]{1,0:T(8,128)(2,1)} %w_ref.1, bf16[512,512]{1,0:T(8,128)(2,1)} %cot_ref.3), custom_call_target="tpu_custom_call" | custom-call | flops 536870912 | bytes 4194304 | tf_op jit(solution)/shard_map/att_grad/pallas_call | solution.py:165
  6.0 1.2 collective-permute-done.rim_ref
  7.2 5.4 %all-to-all-start = ((s16[8,144,512]{2,1,0:T(8,128)(2,1)}), s16[8,144,512]{2,1,0:T(8,128)(2,1)S(1)}, u32[]{:S(2)}, u32[]{:S(2)}) async-start(s16[8,144,512]{2,1,0:T(8,128)(2,1)} %att_grad.1), calls=%async_computation | async-start | bytes 2359296 | tf_op jit(solution)/shard_map/all_to_all | solution.py:876
  13.3 16.1 %forward.1 = (bf16[256,4224]{1,0:T(8,128)(2,1)}, bf16[512,1024]{1,0:T(8,128)(2,1)}, bf16[1024,512]{1,0:T(8,128)(2,1)}, bf16[128,512]{1,0:T(8,128)(2,1)}, bf16[12...) custom-call(s32[1]{0:T(128)} %bitcast.member, ...), custom_call_target="tpu_custom_call" | custom-call | flops 8589934592 | bytes 12582912 | tf_op jit(solution)/shard_map/forward/pallas_call | solution.py:332
  29.3 3.3 %collective-permute-start.3 = (bf16[128,512]{1,0:T(8,128)(2,1)}, bf16[128,512]{1,0:T(8,128)(2,1)S(1)}, u32[]{:S(2)}, u32[]{:S(2)}) collective-permute-start(bf16[128,512]{1,0:T(8,128)(2,1)} %get-tuple-element.54.refs_0_), channel_id=1, source_target_pairs={{0,6},{1,7},{2,0},{3,1},{4,2},{5,3},{6,4},{7,5},{8,14},{9,15},{10,... | collective-permute-start | bytes 393224 | tf_op jit(solution)/shard_map/ppermute | solution.py:884
  32.6 0.9 collective-permute-start.2
  33.5 0.9 collective-permute-start.1
  35.3 11.2 %backward.1 = (s16[16,208,128]{2,1,0:T(8,128)(2,1)}, bf16[304,512]{1,0:T(8,128)(2,1)}) custom-call(s32[8]{0:T(128)} %get-tuple-element.33.bounds, bf16[4096,1024]{1,0:T(8,128)(2,1)} %x_hbm.3, bf16[256,4224]{1,0:T(8,128)(2,1)} %get-tuple-element.34.kv_hbm, bf16[512,1024]{1,0:T(8,128)(2,1)} %get-tuple-element.35.pooled_hbm, bf16[16,1024]{1,0:T(8,128)(2,1)} %copy-done.11, ...), custom_call_target="tpu_custom_call" | custom-call | flops 6442450944 | bytes 16777216 | tf_op jit(solution)/shard_map/backward/pallas_call | solution.py:496
  46.5 9.0 %all-to-all-start.1 = ((s16[16,208,128]{2,1,0:T(8,128)(2,1)}), s16[16,208,128]{2,1,0:T(8,128)(2,1)S(1)}, u32[]{:S(2)}, u32[]{:S(2)}) async-start(s16[16,208,128]{2,1,0:T(8,128)(2,1)} %get-tuple-element.43), calls=%async_computation.1 | async-start | bytes 1703936 | tf_op jit(solution)/shard_map/all_to_all | solution.py:876
  55.7 2.4 %collective-permute-start.9 = (bf16[304,512]{1,0:T(8,128)(2,1)S(1)}, bf16[304,512]{1,0:T(8,128)(2,1)S(1)}, u32[]{:S(2)}, u32[]{:S(2)}) collective-permute-start(bf16[304,512]{1,0:T(8,128)(2,1)S(1)} %copy-done.1), channel_id=1, source_target_pairs={{0,6},{1,7},{2,0},{3,1},{4,2},{5,3},{6,4},{7,5},{8,14},{9,15},{10,... | collective-permute-start | bytes 933896 | tf_op jit(solution)/shard_map/ppermute | solution.py:884
  58.2 2.3 %out_grad.1 = (s16[16,272,128]{2,1,0:T(8,128)(2,1)}, bf16[64,1024]{1,0:T(8,128)(2,1)}) custom-call(s32[1]{0:T(128)} %bitcast.member, bf16[4,128,512]{2,1,0:T(8,128)(2,1)S(1)} %stack.1.mine_ref, bf16[4,128,512]{2,1,0:T(8,128)(2,1)S(1)} %collective-permute-done.12.other_ref, bf16[512,512]{1,0:T(8,128)(2,1)S(1)} %copy-done, s32[1,512]{1,0:T(1,128)S(1)} %copy-done.6), custom_call_target="tpu_custom_call" | custom-call | flops 536870912 | bytes 4194304 | tf_op jit(solution)/shard_map/out_grad/pallas_call | solution.py:558
  60.5 5.0 %collective-permute-done.9.refs_7_ = bf16[304,512]{1,0:T(8,128)(2,1)S(1)} collective-permute-done((bf16[304,512]{1,0:T(8,128)(2,1)S(1)}, bf16[304,512]{1,0:T(8,128)(2,1)S(1)}, u32[]{:S(2)}, u32[]{:S(2)}) %collective-permute-start.9) | collective-permute-done | bytes 311328 | tf_op jit(solution)/shard_map/ppermute | solution.py:884
  65.5 3.3 %collective-permute-done.7.refs_5_ = bf16[304,512]{1,0:T(8,128)(2,1)S(1)} collective-permute-done((bf16[304,512]{1,0:T(8,128)(2,1)S(1)}, bf16[304,512]{1,0:T(8,128)(2,1)S(1)}, u32[]{:S(2)}, u32[]{:S(2)}) %collective-permute-start.7) | collective-permute-done | bytes 311328 | tf_op jit(solution)/shard_map/ppermute | solution.py:884
  68.8 1.3 %all-to-all-done.1.got_ref = s16[16,208,128]{2,1,0:T(8,128)(2,1)S(1)} async-done(((s16[16,208,128]{2,1,0:T(8,128)(2,1)}), s16[16,208,128]{2,1,0:T(8,128)(2,1)S(1)}, u32[]{:S(2)}, u32[]{:S(2)}) %all-to-all-start.1) | async-done | bytes 852000 | tf_op jit(solution)/shard_map/all_to_all | solution.py:876
  70.1 5.9 %all-to-all-start.2 = ((s16[16,272,128]{2,1,0:T(8,128)(2,1)}), s16[16,272,128]{2,1,0:T(8,128)(2,1)}, u32[]{:S(2)}, u32[]{:S(2)}) async-start(s16[16,272,128]{2,1,0:T(8,128)(2,1)} %get-tuple-element.56), calls=%async_computation.2 | async-start | bytes 2228224 | tf_op jit(solution)/shard_map/all_to_all | solution.py:876
  76.1 0.8 collective-permute-start.8
  77.1 1.1 collective-permute-start.4
  78.2 2.7 %collective-permute-start.5 = (bf16[64,128]{1,0:T(8,128)(2,1)S(1)}, bf16[64,128]{1,0:T(8,128)(2,1)S(1)}, u32[]{:S(2)}, u32[]{:S(2)}) collective-permute-start(bf16[64,128]{1,0:T(8,128)(2,1)S(1)} %get-tuple-element.46), channel_id=1, source_target_pairs={{0,4},{1,5},{2,6},{3,7},{4,0},{5,1},{6,2},{7,3},{8,12},{9,13},{10,... | collective-permute-start | bytes 49160 | tf_op jit(solution)/shard_map/ppermute | solution.py:917
  80.8 1.0 collective-permute-start.6
  81.8 4.5 %collective-permute-done.8.refs_6_ = bf16[304,512]{1,0:T(8,128)(2,1)S(1)} collective-permute-done((bf16[304,512]{1,0:T(8,128)(2,1)S(1)}, bf16[304,512]{1,0:T(8,128)(2,1)S(1)}, u32[]{:S(2)}, u32[]{:S(2)}) %collective-permute-start.8) | collective-permute-done | bytes 311328 | tf_op jit(solution)/shard_map/ppermute | solution.py:884
  88.5 2.1 %collective-permute-done.13.other_ref = bf16[128,128]{1,0:T(8,128)(2,1)S(1)} collective-permute-done((bf16[128,128]{1,0:T(8,128)(2,1)S(1)}, bf16[128,128]{1,0:T(8,128)(2,1)S(1)}, u32[]{:S(2)}, u32[]{:S(2)}) %collective-permute-start.13) | collective-permute-done | bytes 32800 | tf_op jit(solution)/shard_map/ppermute | solution.py:889
  90.7 3.3 %all-to-all-done.2.got_ref = s16[16,272,128]{2,1,0:T(8,128)(2,1)} async-done(((s16[16,272,128]{2,1,0:T(8,128)(2,1)}), s16[16,272,128]{2,1,0:T(8,128)(2,1)}, u32[]{:S(2)}, u32[]{:S(2)}) %all-to-all-start.2) | async-done | bytes 1114144 | tf_op jit(solution)/shard_map/all_to_all | solution.py:876
  93.9 2.9 %pack_sums.1 = bf16[16,448,128]{2,1,0:T(8,128)(2,1)} custom-call(s16[16,272,128]{2,1,0:T(8,128)(2,1)} %all-to-all-done.2.got_ref, bf16[128,128]{1,0:T(8,128)(2,1)} %copy-done.4, bf16[128,128]{1,0:T(8,128)(2,1)} %copy-done.10), custom_call_target="tpu_custom_call" | custom-call | flops 1048576 | bytes 3145728 | tf_op jit(solution)/shard_map/pack_sums/pallas_call | solution.py:687
  96.9 4.2 %all-to-all-start.3 = ((bf16[16,448,128]{2,1,0:T(8,128)(2,1)}), bf16[16,448,128]{2,1,0:T(8,128)(2,1)S(1)}, u32[]{:S(2)}, u32[]{:S(2)}) async-start(bf16[16,448,128]{2,1,0:T(8,128)(2,1)} %pack_sums.1), calls=%async_computation.3 | async-start | bytes 3670016 | tf_op jit(solution)/shard_map/all_to_all | solution.py:876
  101.1 1.2 copy-done.7
  102.3 14.1 %byte_grads.1 = (bf16[4096,128]{1,0:T(8,128)(2,1)}, f32[16,128]{1,0:T(8,128)S(1)}, f32[16,128]{1,0:T(8,128)S(1)}) custom-call(s32[1]{0:T(128)} %bitcast.member, s32[8]{0:T(128)S(1)} %copy-done.9, bf16[4,304,512]{2,1,0:T(8,128)(2,1)} %copy-done.5, bf16[4,304,512]{2,1,0:T(8,128)(2,1)} %collective-permute-done.10.other_hbm, bf16[1024,512]{1,0:T(8,128)(2,1)S(1)} %copy-done.7, ...), custom_call_target="tpu_custom_call" | custom-call | flops 8589934592 | bytes 8388608 | tf_op jit(solution)/shard_map/byte_grads/pallas_call | solution.py:842
  116.4 3.8 %collective-permute-start.11 = (f32[16,128]{1,0:T(8,128)S(1)}, f32[16,128]{1,0:T(8,128)S(1)}, u32[]{:S(2)}, u32[]{:S(2)}) collective-permute-start(f32[16,128]{1,0:T(8,128)S(1)} %get-tuple-element.53), channel_id=1, source_target_pairs={{0,8},{8,16},{16,24},{24,32},{32,40},{40,48},{48,56},{56,64},{64,7... | collective-permute-start | bytes 24584 | tf_op jit(solution)/shard_map/ppermute | solution.py:872
  120.2 5.6 %collective-permute-done.11 = f32[16,128]{1,0:T(8,128)S(1)} collective-permute-done((f32[16,128]{1,0:T(8,128)S(1)}, f32[16,128]{1,0:T(8,128)S(1)}, u32[]{:S(2)}, u32[]{:S(2)}) %collective-permute-start.11) | collective-permute-done | bytes 8224 | tf_op jit(solution)/shard_map/ppermute | solution.py:872
  126.5 4.5 %all-to-all-done.3.got_ref = bf16[16,448,128]{2,1,0:T(8,128)(2,1)S(1)} async-done(((bf16[16,448,128]{2,1,0:T(8,128)(2,1)}), bf16[16,448,128]{2,1,0:T(8,128)(2,1)S(1)}, u32[]{:S(2)}, u32[]{:S(2)}) %all-to-all-start.3) | async-done | bytes 1835040 | tf_op jit(solution)/shard_map/all_to_all | solution.py:876
  131.0 2.0 %unpack_sums.1 = (f32[3,128,1024]{2,1,0:T(8,128)}, f32[1024,512]{1,0:T(8,128)}) custom-call(s32[1]{0:T(128)} %bitcast.member, bf16[16,448,128]{2,1,0:T(8,128)(2,1)S(1)} %all-to-all-done.3.got_ref), custom_call_target="tpu_custom_call" | custom-call | flops 1048576 | bytes 6291456 | tf_op jit(solution)/shard_map/unpack_sums/pallas_call | solution.py:733
  (41 shorter events, 4.1 us)
Async XLA Ops:
  1.4 5.8 %collective-permute-start = (bf16[16,1024]{1,0:T(8,128)(2,1)S(1)}, bf16[16,1024]{1,0:T(8,128)(2,1)S(1)}, u32[]{:S(2)}, u32[]{:S(2)}) collective-permute-start(bf16[16,1024]{1,0:T(8,128)(2,1)S(1)} %slice.3), channel_id=1, source_target_pairs={{8,0},{16,8},{24,16},{32,24},{40,32},{48,40},{56,48},{64,56},{72,6... | collective-permute-start | bytes 98312 | tf_op jit(solution)/shard_map/ppermute | solution.py:872
  7.2 6.1 %copy-start.11 = (bf16[16,1024]{1,0:T(8,128)(2,1)}, bf16[16,1024]{1,0:T(8,128)(2,1)S(1)}, u32[]{:S(2)}) copy-start(bf16[16,1024]{1,0:T(8,128)(2,1)S(1)} %collective-permute-done.rim_ref) | copy-start | bytes 98308
  7.2 27.2 %all-to-all-start = ((s16[8,144,512]{2,1,0:T(8,128)(2,1)}), s16[8,144,512]{2,1,0:T(8,128)(2,1)S(1)}, u32[]{:S(2)}, u32[]{:S(2)}) async-start(s16[8,144,512]{2,1,0:T(8,128)(2,1)} %att_grad.1), calls=%async_computation | async-start | bytes 2359296 | tf_op jit(solution)/shard_map/all_to_all | solution.py:876
  29.3 17.2 %collective-permute-start.3 = (bf16[128,512]{1,0:T(8,128)(2,1)}, bf16[128,512]{1,0:T(8,128)(2,1)S(1)}, u32[]{:S(2)}, u32[]{:S(2)}) collective-permute-start(bf16[128,512]{1,0:T(8,128)(2,1)} %get-tuple-element.54.refs_0_), channel_id=1, source_target_pairs={{0,6},{1,7},{2,0},{3,1},{4,2},{5,3},{6,4},{7,5},{8,14},{9,15},{10,... | collective-permute-start | bytes 393224 | tf_op jit(solution)/shard_map/ppermute | solution.py:884
  32.6 13.9 %collective-permute-start.2 = (bf16[128,512]{1,0:T(8,128)(2,1)}, bf16[128,512]{1,0:T(8,128)(2,1)S(1)}, u32[]{:S(2)}, u32[]{:S(2)}) collective-permute-start(bf16[128,512]{1,0:T(8,128)(2,1)} %get-tuple-element.54.refs_0_), channel_id=1, source_target_pairs={{0,4},{1,5},{2,6},{3,7},{4,0},{5,1},{6,2},{7,3},{8,12},{9,13},{10,... | collective-permute-start | bytes 393224 | tf_op jit(solution)/shard_map/ppermute | solution.py:884
  33.5 13.0 %collective-permute-start.1 = (bf16[128,512]{1,0:T(8,128)(2,1)}, bf16[128,512]{1,0:T(8,128)(2,1)S(1)}, u32[]{:S(2)}, u32[]{:S(2)}) collective-permute-start(bf16[128,512]{1,0:T(8,128)(2,1)} %get-tuple-element.54.refs_0_), channel_id=1, source_target_pairs={{0,2},{1,3},{2,4},{3,5},{4,6},{5,7},{6,0},{7,1},{8,10},{9,11},{10,... | collective-permute-start | bytes 393224 | tf_op jit(solution)/shard_map/ppermute | solution.py:884
  34.6 0.7 copy-start.2
  35.3 20.3 %copy-start.3 = (bf16[128,512]{1,0:T(8,128)(2,1)S(1)}, bf16[128,512]{1,0:T(8,128)(2,1)}, u32[]{:S(2)}) copy-start(bf16[128,512]{1,0:T(8,128)(2,1)} %get-tuple-element.54.refs_0_) | copy-start | bytes 393220
  46.5 9.2 %copy-start.1 = (bf16[304,512]{1,0:T(8,128)(2,1)S(1)}, bf16[304,512]{1,0:T(8,128)(2,1)}, u32[]{:S(2)}) copy-start(bf16[304,512]{1,0:T(8,128)(2,1)} %get-tuple-element.48.refs_4_) | copy-start | bytes 933892
  46.5 11.7 %copy-start = (bf16[512,512]{1,0:T(8,128)(2,1)S(1)}, bf16[512,512]{1,0:T(8,128)(2,1)}, u32[]{:S(2)}) copy-start(bf16[512,512]{1,0:T(8,128)(2,1)} %cot_ref.3) | copy-start | bytes 1572868
  46.5 11.7 %copy-start.6 = (s32[1,512]{1,0:T(1,128)S(1)}, s32[1,512]{1,0:T(1,128)}, u32[]{:S(2)}) copy-start(s32[1,512]{1,0:T(1,128)} %owner_ref.1) | copy-start | bytes 6148
  46.5 23.6 %all-to-all-start.1 = ((s16[16,208,128]{2,1,0:T(8,128)(2,1)}), s16[16,208,128]{2,1,0:T(8,128)(2,1)S(1)}, u32[]{:S(2)}, u32[]{:S(2)}) async-start(s16[16,208,128]{2,1,0:T(8,128)(2,1)} %get-tuple-element.43), calls=%async_computation.1 | async-start | bytes 1703936 | tf_op jit(solution)/shard_map/all_to_all | solution.py:876
  55.6 2.5 %collective-permute-start.12 = (bf16[4,128,512]{2,1,0:T(8,128)(2,1)S(1)}, bf16[4,128,512]{2,1,0:T(8,128)(2,1)S(1)}, u32[]{:S(2)}, u32[]{:S(2)}) collective-permute-start(bf16[4,128,512]{2,1,0:T(8,128)(2,1)S(1)} %stack.1.mine_ref), channel_id=1, source_target_pairs={{0,1},{1,0},{2,3},{3,2},{4,5},{5,4},{6,7},{7,6},{8,9},{9,8},{10,11... | collective-permute-start | bytes 1572872 | tf_op jit(solution)/shard_map/ppermute | solution.py:889
  55.7 9.8 %collective-permute-start.9 = (bf16[304,512]{1,0:T(8,128)(2,1)S(1)}, bf16[304,512]{1,0:T(8,128)(2,1)S(1)}, u32[]{:S(2)}, u32[]{:S(2)}) collective-permute-start(bf16[304,512]{1,0:T(8,128)(2,1)S(1)} %copy-done.1), channel_id=1, source_target_pairs={{0,6},{1,7},{2,0},{3,1},{4,2},{5,3},{6,4},{7,5},{8,14},{9,15},{10,... | collective-permute-start | bytes 933896 | tf_op jit(solution)/shard_map/ppermute | solution.py:884
  58.2 10.6 %collective-permute-start.7 = (bf16[304,512]{1,0:T(8,128)(2,1)S(1)}, bf16[304,512]{1,0:T(8,128)(2,1)S(1)}, u32[]{:S(2)}, u32[]{:S(2)}) collective-permute-start(bf16[304,512]{1,0:T(8,128)(2,1)S(1)} %copy-done.1), channel_id=1, source_target_pairs={{0,2},{1,3},{2,4},{3,5},{4,6},{5,7},{6,0},{7,1},{8,10},{9,11},{10,... | collective-permute-start | bytes 933896 | tf_op jit(solution)/shard_map/ppermute | solution.py:884
  70.1 23.8 %all-to-all-start.2 = ((s16[16,272,128]{2,1,0:T(8,128)(2,1)}), s16[16,272,128]{2,1,0:T(8,128)(2,1)}, u32[]{:S(2)}, u32[]{:S(2)}) async-start(s16[16,272,128]{2,1,0:T(8,128)(2,1)} %get-tuple-element.56), calls=%async_computation.2 | async-start | bytes 2228224 | tf_op jit(solution)/shard_map/all_to_all | solution.py:876
  76.1 10.3 %collective-permute-start.8 = (bf16[304,512]{1,0:T(8,128)(2,1)S(1)}, bf16[304,512]{1,0:T(8,128)(2,1)S(1)}, u32[]{:S(2)}, u32[]{:S(2)}) collective-permute-start(bf16[304,512]{1,0:T(8,128)(2,1)S(1)} %copy-done.1), channel_id=1, source_target_pairs={{0,4},{1,5},{2,6},{3,7},{4,0},{5,1},{6,2},{7,3},{8,12},{9,13},{10,... | collective-permute-start | bytes 933896 | tf_op jit(solution)/shard_map/ppermute | solution.py:884
  77.1 9.3 %collective-permute-start.4 = (bf16[64,128]{1,0:T(8,128)(2,1)S(1)}, bf16[64,128]{1,0:T(8,128)(2,1)S(1)}, u32[]{:S(2)}, u32[]{:S(2)}) collective-permute-start(bf16[64,128]{1,0:T(8,128)(2,1)S(1)} %get-tuple-element.45), channel_id=1, source_target_pairs={{0,2},{1,3},{2,0},{3,1},{4,6},{5,7},{6,4},{7,5},{8,10},{9,11},{10,... | collective-permute-start | bytes 49160 | tf_op jit(solution)/shard_map/ppermute | solution.py:917
  78.2 8.5 %collective-permute-start.5 = (bf16[64,128]{1,0:T(8,128)(2,1)S(1)}, bf16[64,128]{1,0:T(8,128)(2,1)S(1)}, u32[]{:S(2)}, u32[]{:S(2)}) collective-permute-start(bf16[64,128]{1,0:T(8,128)(2,1)S(1)} %get-tuple-element.46), channel_id=1, source_target_pairs={{0,4},{1,5},{2,6},{3,7},{4,0},{5,1},{6,2},{7,3},{8,12},{9,13},{10,... | collective-permute-start | bytes 49160 | tf_op jit(solution)/shard_map/ppermute | solution.py:917
  80.8 5.8 %collective-permute-start.6 = (bf16[64,128]{1,0:T(8,128)(2,1)S(1)}, bf16[64,128]{1,0:T(8,128)(2,1)S(1)}, u32[]{:S(2)}, u32[]{:S(2)}) collective-permute-start(bf16[64,128]{1,0:T(8,128)(2,1)S(1)} %get-tuple-element.47), channel_id=1, source_target_pairs={{0,6},{1,7},{2,4},{3,5},{4,2},{5,3},{6,0},{7,1},{8,14},{9,15},{10,... | collective-permute-start | bytes 49160 | tf_op jit(solution)/shard_map/ppermute | solution.py:917
  87.4 0.6 copy-start.4
  88.0 8.9 %copy-start.5 = (bf16[4,304,512]{2,1,0:T(8,128)(2,1)}, bf16[4,304,512]{2,1,0:T(8,128)(2,1)S(1)}, u32[]{:S(2)}) copy-start(bf16[4,304,512]{2,1,0:T(8,128)(2,1)S(1)} %get-tuple-element.49.mine_hbm) | copy-start | bytes 3735556
  88.0 13.0 %collective-permute-start.10 = (bf16[4,304,512]{2,1,0:T(8,128)(2,1)S(1)}, bf16[4,304,512]{2,1,0:T(8,128)(2,1)}, u32[]{:S(2)}, u32[]{:S(2)}) collective-permute-start(bf16[4,304,512]{2,1,0:T(8,128)(2,1)S(1)} %get-tuple-element.49.mine_hbm), channel_id=1, source_target_pairs={{0,1},{1,0},{2,3},{3,2},{4,5},{5,4},{6,7},{7,6},{8,9},{9,8},{10,11... | collective-permute-start | bytes 3735560 | tf_op jit(solution)/shard_map/ppermute | solution.py:889
  88.0 2.6 %collective-permute-start.13 = (bf16[128,128]{1,0:T(8,128)(2,1)S(1)}, bf16[128,128]{1,0:T(8,128)(2,1)S(1)}, u32[]{:S(2)}, u32[]{:S(2)}) collective-permute-start(bf16[128,128]{1,0:T(8,128)(2,1)S(1)} %get-tuple-element.58), channel_id=1, source_target_pairs={{0,1},{1,0},{2,3},{3,2},{4,5},{5,4},{6,7},{7,6},{8,9},{9,8},{10,11... | collective-permute-start | bytes 98312 | tf_op jit(solution)/shard_map/ppermute | solution.py:889
  90.7 3.3 %copy-start.10 = (bf16[128,128]{1,0:T(8,128)(2,1)}, bf16[128,128]{1,0:T(8,128)(2,1)S(1)}, u32[]{:S(2)}) copy-start(bf16[128,128]{1,0:T(8,128)(2,1)S(1)} %collective-permute-done.13.other_ref) | copy-start | bytes 98308
  96.9 4.2 %copy-start.8 = (s32[16,512]{1,0:T(8,128)S(1)}, s32[16,512]{1,0:T(8,128)}, u32[]{:S(2)}) copy-start(s32[16,512]{1,0:T(8,128)} %get-tuple-element.40.row_ref) | copy-start | bytes 98308
  96.9 4.2 %copy-start.9 = (s32[8]{0:T(128)S(1)}, s32[8]{0:T(128)}, u32[]{:S(2)}) copy-start(s32[8]{0:T(128)} %get-tuple-element.33.bounds) | copy-start | bytes 100
  96.9 34.1 %all-to-all-start.3 = ((bf16[16,448,128]{2,1,0:T(8,128)(2,1)}), bf16[16,448,128]{2,1,0:T(8,128)(2,1)S(1)}, u32[]{:S(2)}, u32[]{:S(2)}) async-start(bf16[16,448,128]{2,1,0:T(8,128)(2,1)} %pack_sums.1), calls=%async_computation.3 | async-start | bytes 3670016 | tf_op jit(solution)/shard_map/all_to_all | solution.py:876
  101.1 1.2 copy-start.7
  116.4 9.5 %collective-permute-start.11 = (f32[16,128]{1,0:T(8,128)S(1)}, f32[16,128]{1,0:T(8,128)S(1)}, u32[]{:S(2)}, u32[]{:S(2)}) collective-permute-start(f32[16,128]{1,0:T(8,128)S(1)} %get-tuple-element.53), channel_id=1, source_target_pairs={{0,8},{8,16},{16,24},{24,32},{32,40},{40,48},{48,56},{56,64},{64,7... | collective-permute-start | bytes 24584 | tf_op jit(solution)/shard_map/ppermute | solution.py:872
where the time goes:
time: 134 us; the launch traced here: 133 us
  Pallas kernels  53.2 us (40%)
  starting transfers between devices  43.2 us (32%)
  waiting for transfers between devices  31.2 us (23%)
  local copies, waits for them, and re-layouts  3.28 us (2%)
  between operations  1.73 us (1%)
    all_to_all x4, starting transfers between devices, swap(): return lax.all_to_all(value, axis, split_axis=0, concat_axis=0, tiled=True)  24.5 us
    pallas_call x1, Pallas kernels, forward(): pl.pallas_call(forward_kernel, grid_spec=pltpu.PrefetchScalarGridSpec(num...  16.1 us
    pallas_call x1, Pallas kernels, byte_grads(): pl.pallas_call(bytes_kernel, in_specs=[smem(), smem(), near(), near()] +...  14.1 us
    ppermute x6, waiting for transfers between devices, over_chips(): blocks.append(lax.ppermute(value, 'patch', pairs))  12.8 us
    pallas_call x1, Pallas kernels, backward(): pl.pallas_call(backward_kernel, in_specs=[smem()] + [hbm()] * 3 + [vmem]...  11.2 us
    all_to_all x4, waiting for transfers between devices, swap(): return lax.all_to_all(value, axis, split_axis=0, concat_axis=0, tiled=True)  9.15 us
    ppermute x6, starting transfers between devices, over_chips(): blocks.append(lax.ppermute(value, 'patch', pairs))  8.23 us
    ppermute x2, waiting for transfers between devices, shifted(): lax.ppermute(value, axis, [(source, source + steps) for source in range(f...  6.82 us
  transfers between devices with their start and end apart: 18, of which 10 were waited for; matrix products, arithmetic and copies ran while one was open for 0% of the time, Pallas kernels for 38%

commit v1 on v0

--- a/solution.py
+++ b/solution.py
@@ -350,7 +350,7 @@
                 pltpu.VMEM((patches, LANES), I32),
                 pltpu.VMEM((patches, LANES), F32),
                 pltpu.VMEM((2 * own, patches), F32),
-                pltpu.SemaphoreType.DMA((8,)),
+                pltpu.SemaphoreType.DMA((4,)),
                 pltpu.SemaphoreType.DMA((4,)),
             ],
         ),

time: 134 us -> 133 us (level)
  no operation moved by 1% of the time
where the time goes in v1:
time: 133 us
  Pallas kernels  52.5 us (39%)
  starting transfers between devices  43.2 us (32%)
  waiting for transfers between devices  31.1 us (23%)
  local copies, waits for them, and re-layouts  3.28 us (2%)
  between operations  1.73 us (1%)
    all_to_all x4, starting transfers between devices, swap(): return lax.all_to_all(value, axis, split_axis=0, concat_axis=0, tiled=True)  24.5 us
    pallas_call x1, Pallas kernels, forward(): pl.pallas_call(forward_kernel, grid_spec=pltpu.PrefetchScalarGridSpec(num...  15.4 us
    pallas_call x1, Pallas kernels, byte_grads(): pl.pallas_call(bytes_kernel, in_specs=[smem(), smem(), near(), near()] +...  14.1 us
    ppermute x6, waiting for transfers between devices, over_chips(): blocks.append(lax.ppermute(value, 'patch', pairs))  12.8 us
    pallas_call x1, Pallas kernels, backward(): pl.pallas_call(backward_kernel, in_specs=[smem()] + [hbm()] * 3 + [vmem]...  11.1 us
    all_to_all x4, waiting for transfers between devices, swap(): return lax.all_to_all(value, axis, split_axis=0, concat_axis=0, tiled=True)  9.13 us
    ppermute x6, starting transfers between devices, over_chips(): blocks.append(lax.ppermute(value, 'patch', pairs))  8.2 us
    ppermute x2, waiting for transfers between devices, shifted(): lax.ppermute(value, axis, [(source, source + steps) for source in range(f...  6.8 us
  transfers between devices with their start and end apart: 18, of which 10 were waited for; matrix products, arithmetic and copies ran while one was open for 0% of the time, Pallas kernels for 38%

profile of v1, /device:TPU:0, one launch (start us, length us, event | category | flops | bytes accessed | tf_op | source)
XLA Modules:
  0.0 132.5 jit_solution(947439530027167991)
XLA Ops:
  0.6 0.8 slice.3
  1.4 1.3 collective-permute-start
  2.7 3.3 %att_grad.1 = s16[8,144,512]{2,1,0:T(8,128)(2,1)} custom-call(bf16[1024,512]{1,0:T(8,128)(2,1)} %w_ref.1, bf16[512,512]{1,0:T(8,128)(2,1)} %cot_ref.3), custom_call_target="tpu_custom_call" | custom-call | flops 536870912 | bytes 4194304 | tf_op jit(solution)/shard_map/att_grad/pallas_call | solution.py:165
  6.0 1.2 collective-permute-done.rim_ref
  7.2 5.4 %all-to-all-start = ((s16[8,144,512]{2,1,0:T(8,128)(2,1)}), s16[8,144,512]{2,1,0:T(8,128)(2,1)S(1)}, u32[]{:S(2)}, u32[]{:S(2)}) async-start(s16[8,144,512]{2,1,0:T(8,128)(2,1)} %att_grad.1), calls=%async_computation | async-start | bytes 2359296 | tf_op jit(solution)/shard_map/all_to_all | solution.py:876
  13.3 15.4 %forward.1 = (bf16[256,4224]{1,0:T(8,128)(2,1)}, bf16[512,1024]{1,0:T(8,128)(2,1)}, bf16[1024,512]{1,0:T(8,128)(2,1)}, bf16[128,512]{1,0:T(8,128)(2,1)}, bf16[12...) custom-call(s32[1]{0:T(128)} %bitcast.member, ...), custom_call_target="tpu_custom_call" | custom-call | flops 8589934592 | bytes 12582912 | tf_op jit(solution)/shard_map/forward/pallas_call | solution.py:332
  28.7 3.3 %collective-permute-start.3 = (bf16[128,512]{1,0:T(8,128)(2,1)}, bf16[128,512]{1,0:T(8,128)(2,1)S(1)}, u32[]{:S(2)}, u32[]{:S(2)}) collective-permute-start(bf16[128,512]{1,0:T(8,128)(2,1)} %get-tuple-element.54.refs_0_), channel_id=1, source_target_pairs={{0,6},{1,7},{2,0},{3,1},{4,2},{5,3},{6,4},{7,5},{8,14},{9,15},{10,... | collective-permute-start | bytes 393224 | tf_op jit(solution)/shard_map/ppermute | solution.py:884
  32.0 0.8 collective-permute-start.2
  32.8 0.9 collective-permute-start.1
  34.7 11.1 %backward.1 = (s16[16,208,128]{2,1,0:T(8,128)(2,1)}, bf16[304,512]{1,0:T(8,128)(2,1)}) custom-call(s32[8]{0:T(128)} %get-tuple-element.33.bounds, bf16[4096,1024]{1,0:T(8,128)(2,1)} %x_hbm.3, bf16[256,4224]{1,0:T(8,128)(2,1)} %get-tuple-element.34.kv_hbm, bf16[512,1024]{1,0:T(8,128)(2,1)} %get-tuple-element.35.pooled_hbm, bf16[16,1024]{1,0:T(8,128)(2,1)} %copy-done.11, ...), custom_call_target="tpu_custom_call" | custom-call | flops 6442450944 | bytes 16777216 | tf_op jit(solution)/shard_map/backward/pallas_call | solution.py:496
  45.9 9.0 %all-to-all-start.1 = ((s16[16,208,128]{2,1,0:T(8,128)(2,1)}), s16[16,208,128]{2,1,0:T(8,128)(2,1)S(1)}, u32[]{:S(2)}, u32[]{:S(2)}) async-start(s16[16,208,128]{2,1,0:T(8,128)(2,1)} %get-tuple-element.43), calls=%async_computation.1 | async-start | bytes 1703936 | tf_op jit(solution)/shard_map/all_to_all | solution.py:876
  55.1 2.4 %collective-permute-start.9 = (bf16[304,512]{1,0:T(8,128)(2,1)S(1)}, bf16[304,512]{1,0:T(8,128)(2,1)S(1)}, u32[]{:S(2)}, u32[]{:S(2)}) collective-permute-start(bf16[304,512]{1,0:T(8,128)(2,1)S(1)} %copy-done.1), channel_id=1, source_target_pairs={{0,6},{1,7},{2,0},{3,1},{4,2},{5,3},{6,4},{7,5},{8,14},{9,15},{10,... | collective-permute-start | bytes 933896 | tf_op jit(solution)/shard_map/ppermute | solution.py:884
  57.5 2.3 %out_grad.1 = (s16[16,272,128]{2,1,0:T(8,128)(2,1)}, bf16[64,1024]{1,0:T(8,128)(2,1)}) custom-call(s32[1]{0:T(128)} %bitcast.member, bf16[4,128,512]{2,1,0:T(8,128)(2,1)S(1)} %stack.1.mine_ref, bf16[4,128,512]{2,1,0:T(8,128)(2,1)S(1)} %collective-permute-done.12.other_ref, bf16[512,512]{1,0:T(8,128)(2,1)S(1)} %copy-done, s32[1,512]{1,0:T(1,128)S(1)} %copy-done.6), custom_call_target="tpu_custom_call" | custom-call | flops 536870912 | bytes 4194304 | tf_op jit(solution)/shard_map/out_grad/pallas_call | solution.py:558
  59.9 5.0 %collective-permute-done.9.refs_7_ = bf16[304,512]{1,0:T(8,128)(2,1)S(1)} collective-permute-done((bf16[304,512]{1,0:T(8,128)(2,1)S(1)}, bf16[304,512]{1,0:T(8,128)(2,1)S(1)}, u32[]{:S(2)}, u32[]{:S(2)}) %collective-permute-start.9) | collective-permute-done | bytes 311328 | tf_op jit(solution)/shard_map/ppermute | solution.py:884
  64.9 3.3 %collective-permute-done.7.refs_5_ = bf16[304,512]{1,0:T(8,128)(2,1)S(1)} collective-permute-done((bf16[304,512]{1,0:T(8,128)(2,1)S(1)}, bf16[304,512]{1,0:T(8,128)(2,1)S(1)}, u32[]{:S(2)}, u32[]{:S(2)}) %collective-permute-start.7) | collective-permute-done | bytes 311328 | tf_op jit(solution)/shard_map/ppermute | solution.py:884
  68.2 1.3 all-to-all-done.1.got_ref
  69.5 5.9 %all-to-all-start.2 = ((s16[16,272,128]{2,1,0:T(8,128)(2,1)}), s16[16,272,128]{2,1,0:T(8,128)(2,1)}, u32[]{:S(2)}, u32[]{:S(2)}) async-start(s16[16,272,128]{2,1,0:T(8,128)(2,1)} %get-tuple-element.56), calls=%async_computation.2 | async-start | bytes 2228224 | tf_op jit(solution)/shard_map/all_to_all | solution.py:876
  75.4 0.7 collective-permute-start.8
  76.4 1.1 collective-permute-start.4
  77.5 2.7 %collective-permute-start.5 = (bf16[64,128]{1,0:T(8,128)(2,1)S(1)}, bf16[64,128]{1,0:T(8,128)(2,1)S(1)}, u32[]{:S(2)}, u32[]{:S(2)}) collective-permute-start(bf16[64,128]{1,0:T(8,128)(2,1)S(1)} %get-tuple-element.46), channel_id=1, source_target_pairs={{0,4},{1,5},{2,6},{3,7},{4,0},{5,1},{6,2},{7,3},{8,12},{9,13},{10,... | collective-permute-start | bytes 49160 | tf_op jit(solution)/shard_map/ppermute | solution.py:917
  80.2 1.0 collective-permute-start.6
  81.2 4.5 %collective-permute-done.8.refs_6_ = bf16[304,512]{1,0:T(8,128)(2,1)S(1)} collective-permute-done((bf16[304,512]{1,0:T(8,128)(2,1)S(1)}, bf16[304,512]{1,0:T(8,128)(2,1)S(1)}, u32[]{:S(2)}, u32[]{:S(2)}) %collective-permute-start.8) | collective-permute-done | bytes 311328 | tf_op jit(solution)/shard_map/ppermute | solution.py:884
  87.9 2.1 %collective-permute-done.13.other_ref = bf16[128,128]{1,0:T(8,128)(2,1)S(1)} collective-permute-done((bf16[128,128]{1,0:T(8,128)(2,1)S(1)}, bf16[128,128]{1,0:T(8,128)(2,1)S(1)}, u32[]{:S(2)}, u32[]{:S(2)}) %collective-permute-start.13) | collective-permute-done | bytes 32800 | tf_op jit(solution)/shard_map/ppermute | solution.py:889
  90.0 3.3 %all-to-all-done.2.got_ref = s16[16,272,128]{2,1,0:T(8,128)(2,1)} async-done(((s16[16,272,128]{2,1,0:T(8,128)(2,1)}), s16[16,272,128]{2,1,0:T(8,128)(2,1)}, u32[]{:S(2)}, u32[]{:S(2)}) %all-to-all-start.2) | async-done | bytes 1114144 | tf_op jit(solution)/shard_map/all_to_all | solution.py:876
  93.3 2.9 %pack_sums.1 = bf16[16,448,128]{2,1,0:T(8,128)(2,1)} custom-call(s16[16,272,128]{2,1,0:T(8,128)(2,1)} %all-to-all-done.2.got_ref, bf16[128,128]{1,0:T(8,128)(2,1)} %copy-done.4, bf16[128,128]{1,0:T(8,128)(2,1)} %copy-done.10), custom_call_target="tpu_custom_call" | custom-call | flops 1048576 | bytes 3145728 | tf_op jit(solution)/shard_map/pack_sums/pallas_call | solution.py:687
  96.3 4.2 %all-to-all-start.3 = ((bf16[16,448,128]{2,1,0:T(8,128)(2,1)}), bf16[16,448,128]{2,1,0:T(8,128)(2,1)S(1)}, u32[]{:S(2)}, u32[]{:S(2)}) async-start(bf16[16,448,128]{2,1,0:T(8,128)(2,1)} %pack_sums.1), calls=%async_computation.3 | async-start | bytes 3670016 | tf_op jit(solution)/shard_map/all_to_all | solution.py:876
  100.5 1.2 copy-done.7
  101.7 14.1 %byte_grads.1 = (bf16[4096,128]{1,0:T(8,128)(2,1)}, f32[16,128]{1,0:T(8,128)S(1)}, f32[16,128]{1,0:T(8,128)S(1)}) custom-call(s32[1]{0:T(128)} %bitcast.member, s32[8]{0:T(128)S(1)} %copy-done.9, bf16[4,304,512]{2,1,0:T(8,128)(2,1)} %copy-done.5, bf16[4,304,512]{2,1,0:T(8,128)(2,1)} %collective-permute-done.10.other_hbm, bf16[1024,512]{1,0:T(8,128)(2,1)S(1)} %copy-done.7, ...), custom_call_target="tpu_custom_call" | custom-call | flops 8589934592 | bytes 8388608 | tf_op jit(solution)/shard_map/byte_grads/pallas_call | solution.py:842
  115.8 3.8 %collective-permute-start.11 = (f32[16,128]{1,0:T(8,128)S(1)}, f32[16,128]{1,0:T(8,128)S(1)}, u32[]{:S(2)}, u32[]{:S(2)}) collective-permute-start(f32[16,128]{1,0:T(8,128)S(1)} %get-tuple-element.53), channel_id=1, source_target_pairs={{0,8},{8,16},{16,24},{24,32},{32,40},{40,48},{48,56},{56,64},{64,7... | collective-permute-start | bytes 24584 | tf_op jit(solution)/shard_map/ppermute | solution.py:872
  119.6 5.6 %collective-permute-done.11 = f32[16,128]{1,0:T(8,128)S(1)} collective-permute-done((f32[16,128]{1,0:T(8,128)S(1)}, f32[16,128]{1,0:T(8,128)S(1)}, u32[]{:S(2)}, u32[]{:S(2)}) %collective-permute-start.11) | collective-permute-done | bytes 8224 | tf_op jit(solution)/shard_map/ppermute | solution.py:872
  125.8 4.5 %all-to-all-done.3.got_ref = bf16[16,448,128]{2,1,0:T(8,128)(2,1)S(1)} async-done(((bf16[16,448,128]{2,1,0:T(8,128)(2,1)}), bf16[16,448,128]{2,1,0:T(8,128)(2,1)S(1)}, u32[]{:S(2)}, u32[]{:S(2)}) %all-to-all-start.3) | async-done | bytes 1835040 | tf_op jit(solution)/shard_map/all_to_all | solution.py:876
  130.4 2.0 %unpack_sums.1 = (f32[3,128,1024]{2,1,0:T(8,128)}, f32[1024,512]{1,0:T(8,128)}) custom-call(s32[1]{0:T(128)} %bitcast.member, bf16[16,448,128]{2,1,0:T(8,128)(2,1)S(1)} %all-to-all-done.3.got_ref), custom_call_target="tpu_custom_call" | custom-call | flops 1048576 | bytes 6291456 | tf_op jit(solution)/shard_map/unpack_sums/pallas_call | solution.py:733
  (41 shorter events, 4.1 us)
Async XLA Ops:
  1.4 5.8 %collective-permute-start = (bf16[16,1024]{1,0:T(8,128)(2,1)S(1)}, bf16[16,1024]{1,0:T(8,128)(2,1)S(1)}, u32[]{:S(2)}, u32[]{:S(2)}) collective-permute-start(bf16[16,1024]{1,0:T(8,128)(2,1)S(1)} %slice.3), channel_id=1, source_target_pairs={{8,0},{16,8},{24,16},{32,24},{40,32},{48,40},{56,48},{64,56},{72,6... | collective-permute-start | bytes 98312 | tf_op jit(solution)/shard_map/ppermute | solution.py:872
  7.2 6.1 %copy-start.11 = (bf16[16,1024]{1,0:T(8,128)(2,1)}, bf16[16,1024]{1,0:T(8,128)(2,1)S(1)}, u32[]{:S(2)}) copy-start(bf16[16,1024]{1,0:T(8,128)(2,1)S(1)} %collective-permute-done.rim_ref) | copy-start | bytes 98308
  7.2 26.5 %all-to-all-start = ((s16[8,144,512]{2,1,0:T(8,128)(2,1)}), s16[8,144,512]{2,1,0:T(8,128)(2,1)S(1)}, u32[]{:S(2)}, u32[]{:S(2)}) async-start(s16[8,144,512]{2,1,0:T(8,128)(2,1)} %att_grad.1), calls=%async_computation | async-start | bytes 2359296 | tf_op jit(solution)/shard_map/all_to_all | solution.py:876
  28.7 17.2 %collective-permute-start.3 = (bf16[128,512]{1,0:T(8,128)(2,1)}, bf16[128,512]{1,0:T(8,128)(2,1)S(1)}, u32[]{:S(2)}, u32[]{:S(2)}) collective-permute-start(bf16[128,512]{1,0:T(8,128)(2,1)} %get-tuple-element.54.refs_0_), channel_id=1, source_target_pairs={{0,6},{1,7},{2,0},{3,1},{4,2},{5,3},{6,4},{7,5},{8,14},{9,15},{10,... | collective-permute-start | bytes 393224 | tf_op jit(solution)/shard_map/ppermute | solution.py:884
  32.0 13.9 %collective-permute-start.2 = (bf16[128,512]{1,0:T(8,128)(2,1)}, bf16[128,512]{1,0:T(8,128)(2,1)S(1)}, u32[]{:S(2)}, u32[]{:S(2)}) collective-permute-start(bf16[128,512]{1,0:T(8,128)(2,1)} %get-tuple-element.54.refs_0_), channel_id=1, source_target_pairs={{0,4},{1,5},{2,6},{3,7},{4,0},{5,1},{6,2},{7,3},{8,12},{9,13},{10,... | collective-permute-start | bytes 393224 | tf_op jit(solution)/shard_map/ppermute | solution.py:884
  32.8 13.0 %collective-permute-start.1 = (bf16[128,512]{1,0:T(8,128)(2,1)}, bf16[128,512]{1,0:T(8,128)(2,1)S(1)}, u32[]{:S(2)}, u32[]{:S(2)}) collective-permute-start(bf16[128,512]{1,0:T(8,128)(2,1)} %get-tuple-element.54.refs_0_), channel_id=1, source_target_pairs={{0,2},{1,3},{2,4},{3,5},{4,6},{5,7},{6,0},{7,1},{8,10},{9,11},{10,... | collective-permute-start | bytes 393224 | tf_op jit(solution)/shard_map/ppermute | solution.py:884
  34.0 0.7 copy-start.2
  34.7 20.3 %copy-start.3 = (bf16[128,512]{1,0:T(8,128)(2,1)S(1)}, bf16[128,512]{1,0:T(8,128)(2,1)}, u32[]{:S(2)}) copy-start(bf16[128,512]{1,0:T(8,128)(2,1)} %get-tuple-element.54.refs_0_) | copy-start | bytes 393220
  45.8 9.3 %copy-start.1 = (bf16[304,512]{1,0:T(8,128)(2,1)S(1)}, bf16[304,512]{1,0:T(8,128)(2,1)}, u32[]{:S(2)}) copy-start(bf16[304,512]{1,0:T(8,128)(2,1)} %get-tuple-element.48.refs_4_) | copy-start | bytes 933892
  45.8 11.7 %copy-start = (bf16[512,512]{1,0:T(8,128)(2,1)S(1)}, bf16[512,512]{1,0:T(8,128)(2,1)}, u32[]{:S(2)}) copy-start(bf16[512,512]{1,0:T(8,128)(2,1)} %cot_ref.3) | copy-start | bytes 1572868
  45.8 11.7 %copy-start.6 = (s32[1,512]{1,0:T(1,128)S(1)}, s32[1,512]{1,0:T(1,128)}, u32[]{:S(2)}) copy-start(s32[1,512]{1,0:T(1,128)} %owner_ref.1) | copy-start | bytes 6148
  45.9 23.6 %all-to-all-start.1 = ((s16[16,208,128]{2,1,0:T(8,128)(2,1)}), s16[16,208,128]{2,1,0:T(8,128)(2,1)S(1)}, u32[]{:S(2)}, u32[]{:S(2)}) async-start(s16[16,208,128]{2,1,0:T(8,128)(2,1)} %get-tuple-element.43), calls=%async_computation.1 | async-start | bytes 1703936 | tf_op jit(solution)/shard_map/all_to_all | solution.py:876
  55.0 2.6 %collective-permute-start.12 = (bf16[4,128,512]{2,1,0:T(8,128)(2,1)S(1)}, bf16[4,128,512]{2,1,0:T(8,128)(2,1)S(1)}, u32[]{:S(2)}, u32[]{:S(2)}) collective-permute-start(bf16[4,128,512]{2,1,0:T(8,128)(2,1)S(1)} %stack.1.mine_ref), channel_id=1, source_target_pairs={{0,1},{1,0},{2,3},{3,2},{4,5},{5,4},{6,7},{7,6},{8,9},{9,8},{10,11... | collective-permute-start | bytes 1572872 | tf_op jit(solution)/shard_map/ppermute | solution.py:889
  55.1 9.8 %collective-permute-start.9 = (bf16[304,512]{1,0:T(8,128)(2,1)S(1)}, bf16[304,512]{1,0:T(8,128)(2,1)S(1)}, u32[]{:S(2)}, u32[]{:S(2)}) collective-permute-start(bf16[304,512]{1,0:T(8,128)(2,1)S(1)} %copy-done.1), channel_id=1, source_target_pairs={{0,6},{1,7},{2,0},{3,1},{4,2},{5,3},{6,4},{7,5},{8,14},{9,15},{10,... | collective-permute-start | bytes 933896 | tf_op jit(solution)/shard_map/ppermute | solution.py:884
  57.5 10.6 %collective-permute-start.7 = (bf16[304,512]{1,0:T(8,128)(2,1)S(1)}, bf16[304,512]{1,0:T(8,128)(2,1)S(1)}, u32[]{:S(2)}, u32[]{:S(2)}) collective-permute-start(bf16[304,512]{1,0:T(8,128)(2,1)S(1)} %copy-done.1), channel_id=1, source_target_pairs={{0,2},{1,3},{2,4},{3,5},{4,6},{5,7},{6,0},{7,1},{8,10},{9,11},{10,... | collective-permute-start | bytes 933896 | tf_op jit(solution)/shard_map/ppermute | solution.py:884
  69.5 23.8 %all-to-all-start.2 = ((s16[16,272,128]{2,1,0:T(8,128)(2,1)}), s16[16,272,128]{2,1,0:T(8,128)(2,1)}, u32[]{:S(2)}, u32[]{:S(2)}) async-start(s16[16,272,128]{2,1,0:T(8,128)(2,1)} %get-tuple-element.56), calls=%async_computation.2 | async-start | bytes 2228224 | tf_op jit(solution)/shard_map/all_to_all | solution.py:876
  75.4 10.3 %collective-permute-start.8 = (bf16[304,512]{1,0:T(8,128)(2,1)S(1)}, bf16[304,512]{1,0:T(8,128)(2,1)S(1)}, u32[]{:S(2)}, u32[]{:S(2)}) collective-permute-start(bf16[304,512]{1,0:T(8,128)(2,1)S(1)} %copy-done.1), channel_id=1, source_target_pairs={{0,4},{1,5},{2,6},{3,7},{4,0},{5,1},{6,2},{7,3},{8,12},{9,13},{10,... | collective-permute-start | bytes 933896 | tf_op jit(solution)/shard_map/ppermute | solution.py:884
  76.4 9.3 %collective-permute-start.4 = (bf16[64,128]{1,0:T(8,128)(2,1)S(1)}, bf16[64,128]{1,0:T(8,128)(2,1)S(1)}, u32[]{:S(2)}, u32[]{:S(2)}) collective-permute-start(bf16[64,128]{1,0:T(8,128)(2,1)S(1)} %get-tuple-element.45), channel_id=1, source_target_pairs={{0,2},{1,3},{2,0},{3,1},{4,6},{5,7},{6,4},{7,5},{8,10},{9,11},{10,... | collective-permute-start | bytes 49160 | tf_op jit(solution)/shard_map/ppermute | solution.py:917
  77.5 8.5 %collective-permute-start.5 = (bf16[64,128]{1,0:T(8,128)(2,1)S(1)}, bf16[64,128]{1,0:T(8,128)(2,1)S(1)}, u32[]{:S(2)}, u32[]{:S(2)}) collective-permute-start(bf16[64,128]{1,0:T(8,128)(2,1)S(1)} %get-tuple-element.46), channel_id=1, source_target_pairs={{0,4},{1,5},{2,6},{3,7},{4,0},{5,1},{6,2},{7,3},{8,12},{9,13},{10,... | collective-permute-start | bytes 49160 | tf_op jit(solution)/shard_map/ppermute | solution.py:917
  80.2 5.8 %collective-permute-start.6 = (bf16[64,128]{1,0:T(8,128)(2,1)S(1)}, bf16[64,128]{1,0:T(8,128)(2,1)S(1)}, u32[]{:S(2)}, u32[]{:S(2)}) collective-permute-start(bf16[64,128]{1,0:T(8,128)(2,1)S(1)} %get-tuple-element.47), channel_id=1, source_target_pairs={{0,6},{1,7},{2,4},{3,5},{4,2},{5,3},{6,0},{7,1},{8,14},{9,15},{10,... | collective-permute-start | bytes 49160 | tf_op jit(solution)/shard_map/ppermute | solution.py:917
  86.8 0.6 copy-start.4
  87.4 8.9 %copy-start.5 = (bf16[4,304,512]{2,1,0:T(8,128)(2,1)}, bf16[4,304,512]{2,1,0:T(8,128)(2,1)S(1)}, u32[]{:S(2)}) copy-start(bf16[4,304,512]{2,1,0:T(8,128)(2,1)S(1)} %get-tuple-element.49.mine_hbm) | copy-start | bytes 3735556
  87.4 13.0 %collective-permute-start.10 = (bf16[4,304,512]{2,1,0:T(8,128)(2,1)S(1)}, bf16[4,304,512]{2,1,0:T(8,128)(2,1)}, u32[]{:S(2)}, u32[]{:S(2)}) collective-permute-start(bf16[4,304,512]{2,1,0:T(8,128)(2,1)S(1)} %get-tuple-element.49.mine_hbm), channel_id=1, source_target_pairs={{0,1},{1,0},{2,3},{3,2},{4,5},{5,4},{6,7},{7,6},{8,9},{9,8},{10,11... | collective-permute-start | bytes 3735560 | tf_op jit(solution)/shard_map/ppermute | solution.py:889
  87.4 2.6 %collective-permute-start.13 = (bf16[128,128]{1,0:T(8,128)(2,1)S(1)}, bf16[128,128]{1,0:T(8,128)(2,1)S(1)}, u32[]{:S(2)}, u32[]{:S(2)}) collective-permute-start(bf16[128,128]{1,0:T(8,128)(2,1)S(1)} %get-tuple-element.58), channel_id=1, source_target_pairs={{0,1},{1,0},{2,3},{3,2},{4,5},{5,4},{6,7},{7,6},{8,9},{9,8},{10,11... | collective-permute-start | bytes 98312 | tf_op jit(solution)/shard_map/ppermute | solution.py:889
  90.0 3.3 %copy-start.10 = (bf16[128,128]{1,0:T(8,128)(2,1)}, bf16[128,128]{1,0:T(8,128)(2,1)S(1)}, u32[]{:S(2)}) copy-start(bf16[128,128]{1,0:T(8,128)(2,1)S(1)} %collective-permute-done.13.other_ref) | copy-start | bytes 98308
  96.2 4.2 %copy-start.8 = (s32[16,512]{1,0:T(8,128)S(1)}, s32[16,512]{1,0:T(8,128)}, u32[]{:S(2)}) copy-start(s32[16,512]{1,0:T(8,128)} %get-tuple-element.40.row_ref) | copy-start | bytes 98308
  96.2 4.2 %copy-start.9 = (s32[8]{0:T(128)S(1)}, s32[8]{0:T(128)}, u32[]{:S(2)}) copy-start(s32[8]{0:T(128)} %get-tuple-element.33.bounds) | copy-start | bytes 100
  96.3 34.1 %all-to-all-start.3 = ((bf16[16,448,128]{2,1,0:T(8,128)(2,1)}), bf16[16,448,128]{2,1,0:T(8,128)(2,1)S(1)}, u32[]{:S(2)}, u32[]{:S(2)}) async-start(bf16[16,448,128]{2,1,0:T(8,128)(2,1)} %pack_sums.1), calls=%async_computation.3 | async-start | bytes 3670016 | tf_op jit(solution)/shard_map/all_to_all | solution.py:876
  100.5 1.2 copy-start.7
  115.8 9.5 %collective-permute-start.11 = (f32[16,128]{1,0:T(8,128)S(1)}, f32[16,128]{1,0:T(8,128)S(1)}, u32[]{:S(2)}, u32[]{:S(2)}) collective-permute-start(f32[16,128]{1,0:T(8,128)S(1)} %get-tuple-element.53), channel_id=1, source_target_pairs={{0,8},{8,16},{16,24},{24,32},{32,40},{40,48},{48,56},{56,64},{64,7... | collective-permute-start | bytes 24584 | tf_op jit(solution)/shard_map/ppermute | solution.py:872

commit v2 on v1

--- a/solution.py
+++ b/solution.py
@@ -100,7 +100,7 @@
 
     @pl.when(bounds[blocks + 1] == 0)
     def _():
-        loop(TILE, UNROLL)
+        loop(TILE, 2 * UNROLL)
 
     @pl.when(bounds[blocks + 1] > 0)
     def _():

time: 133 us -> 133 us (level)
  no operation moved by 1% of the time
where the time goes in v2:
time: 133 us; the launch traced here: 132 us
  Pallas kernels  52 us (39%)
  starting transfers between devices  43.2 us (32%)
  waiting for transfers between devices  31.1 us (23%)
  local copies, waits for them, and re-layouts  3.28 us (2%)
  between operations  1.73 us (1%)
    all_to_all x4, starting transfers between devices, swap(): return lax.all_to_all(value, axis, split_axis=0, concat_axis=0, tiled=True)  24.5 us
    pallas_call x1, Pallas kernels, forward(): pl.pallas_call(forward_kernel, grid_spec=pltpu.PrefetchScalarGridSpec(num...  15.2 us
    pallas_call x1, Pallas kernels, byte_grads(): pl.pallas_call(bytes_kernel, in_specs=[smem(), smem(), near(), near()] +...  14 us
    ppermute x6, waiting for transfers between devices, over_chips(): blocks.append(lax.ppermute(value, 'patch', pairs))  12.8 us
    pallas_call x1, Pallas kernels, backward(): pl.pallas_call(backward_kernel, in_specs=[smem()] + [hbm()] * 3 + [vmem]...  10.9 us
    all_to_all x4, waiting for transfers between devices, swap(): return lax.all_to_all(value, axis, split_axis=0, concat_axis=0, tiled=True)  9.15 us
    ppermute x6, starting transfers between devices, over_chips(): blocks.append(lax.ppermute(value, 'patch', pairs))  8.22 us
    ppermute x2, waiting for transfers between devices, shifted(): lax.ppermute(value, axis, [(source, source + steps) for source in range(f...  6.8 us
  transfers between devices with their start and end apart: 18, of which 10 were waited for; matrix products, arithmetic and copies ran while one was open for 0% of the time, Pallas kernels for 38%

profile of v2, /device:TPU:0, one launch (start us, length us, event | category | flops | bytes accessed | tf_op | source)
XLA Modules:
  0.0 132.0 jit_solution(15682826310034414415)
XLA Ops:
  0.6 0.8 slice.3
  1.4 1.3 collective-permute-start
  2.7 3.3 %att_grad.1 = s16[8,144,512]{2,1,0:T(8,128)(2,1)} custom-call(bf16[1024,512]{1,0:T(8,128)(2,1)} %w_ref.1, bf16[512,512]{1,0:T(8,128)(2,1)} %cot_ref.3), custom_call_target="tpu_custom_call" | custom-call | flops 536870912 | bytes 4194304 | tf_op jit(solution)/shard_map/att_grad/pallas_call | solution.py:165
  6.0 1.2 collective-permute-done.rim_ref
  7.2 5.4 %all-to-all-start = ((s16[8,144,512]{2,1,0:T(8,128)(2,1)}), s16[8,144,512]{2,1,0:T(8,128)(2,1)S(1)}, u32[]{:S(2)}, u32[]{:S(2)}) async-start(s16[8,144,512]{2,1,0:T(8,128)(2,1)} %att_grad.1), calls=%async_computation | async-start | bytes 2359296 | tf_op jit(solution)/shard_map/all_to_all | solution.py:876
  13.3 15.2 %forward.1 = (bf16[256,4224]{1,0:T(8,128)(2,1)}, bf16[512,1024]{1,0:T(8,128)(2,1)}, bf16[1024,512]{1,0:T(8,128)(2,1)}, bf16[128,512]{1,0:T(8,128)(2,1)}, bf16[12...) custom-call(s32[1]{0:T(128)} %bitcast.member, ...), custom_call_target="tpu_custom_call" | custom-call | flops 8589934592 | bytes 12582912 | tf_op jit(solution)/shard_map/forward/pallas_call | solution.py:332
  28.4 3.3 %collective-permute-start.3 = (bf16[128,512]{1,0:T(8,128)(2,1)}, bf16[128,512]{1,0:T(8,128)(2,1)S(1)}, u32[]{:S(2)}, u32[]{:S(2)}) collective-permute-start(bf16[128,512]{1,0:T(8,128)(2,1)} %get-tuple-element.54.refs_0_), channel_id=1, source_target_pairs={{0,6},{1,7},{2,0},{3,1},{4,2},{5,3},{6,4},{7,5},{8,14},{9,15},{10,... | collective-permute-start | bytes 393224 | tf_op jit(solution)/shard_map/ppermute | solution.py:884
  31.7 0.8 collective-permute-start.2
  32.6 0.9 collective-permute-start.1
  34.4 10.9 %backward.1 = (s16[16,208,128]{2,1,0:T(8,128)(2,1)}, bf16[304,512]{1,0:T(8,128)(2,1)}) custom-call(s32[8]{0:T(128)} %get-tuple-element.33.bounds, bf16[4096,1024]{1,0:T(8,128)(2,1)} %x_hbm.3, bf16[256,4224]{1,0:T(8,128)(2,1)} %get-tuple-element.34.kv_hbm, bf16[512,1024]{1,0:T(8,128)(2,1)} %get-tuple-element.35.pooled_hbm, bf16[16,1024]{1,0:T(8,128)(2,1)} %copy-done.11, ...), custom_call_target="tpu_custom_call" | custom-call | flops 6442450944 | bytes 16777216 | tf_op jit(solution)/shard_map/backward/pallas_call | solution.py:496
  45.4 9.0 %all-to-all-start.1 = ((s16[16,208,128]{2,1,0:T(8,128)(2,1)}), s16[16,208,128]{2,1,0:T(8,128)(2,1)S(1)}, u32[]{:S(2)}, u32[]{:S(2)}) async-start(s16[16,208,128]{2,1,0:T(8,128)(2,1)} %get-tuple-element.43), calls=%async_computation.1 | async-start | bytes 1703936 | tf_op jit(solution)/shard_map/all_to_all | solution.py:876
  54.6 2.4 %collective-permute-start.9 = (bf16[304,512]{1,0:T(8,128)(2,1)S(1)}, bf16[304,512]{1,0:T(8,128)(2,1)S(1)}, u32[]{:S(2)}, u32[]{:S(2)}) collective-permute-start(bf16[304,512]{1,0:T(8,128)(2,1)S(1)} %copy-done.1), channel_id=1, source_target_pairs={{0,6},{1,7},{2,0},{3,1},{4,2},{5,3},{6,4},{7,5},{8,14},{9,15},{10,... | collective-permute-start | bytes 933896 | tf_op jit(solution)/shard_map/ppermute | solution.py:884
  57.0 2.3 %out_grad.1 = (s16[16,272,128]{2,1,0:T(8,128)(2,1)}, bf16[64,1024]{1,0:T(8,128)(2,1)}) custom-call(s32[1]{0:T(128)} %bitcast.member, bf16[4,128,512]{2,1,0:T(8,128)(2,1)S(1)} %stack.1.mine_ref, bf16[4,128,512]{2,1,0:T(8,128)(2,1)S(1)} %collective-permute-done.12.other_ref, bf16[512,512]{1,0:T(8,128)(2,1)S(1)} %copy-done, s32[1,512]{1,0:T(1,128)S(1)} %copy-done.6), custom_call_target="tpu_custom_call" | custom-call | flops 536870912 | bytes 4194304 | tf_op jit(solution)/shard_map/out_grad/pallas_call | solution.py:558
  59.4 5.0 %collective-permute-done.9.refs_7_ = bf16[304,512]{1,0:T(8,128)(2,1)S(1)} collective-permute-done((bf16[304,512]{1,0:T(8,128)(2,1)S(1)}, bf16[304,512]{1,0:T(8,128)(2,1)S(1)}, u32[]{:S(2)}, u32[]{:S(2)}) %collective-permute-start.9) | collective-permute-done | bytes 311328 | tf_op jit(solution)/shard_map/ppermute | solution.py:884
  64.4 3.3 %collective-permute-done.7.refs_5_ = bf16[304,512]{1,0:T(8,128)(2,1)S(1)} collective-permute-done((bf16[304,512]{1,0:T(8,128)(2,1)S(1)}, bf16[304,512]{1,0:T(8,128)(2,1)S(1)}, u32[]{:S(2)}, u32[]{:S(2)}) %collective-permute-start.7) | collective-permute-done | bytes 311328 | tf_op jit(solution)/shard_map/ppermute | solution.py:884
  67.6 1.3 %all-to-all-done.1.got_ref = s16[16,208,128]{2,1,0:T(8,128)(2,1)S(1)} async-done(((s16[16,208,128]{2,1,0:T(8,128)(2,1)}), s16[16,208,128]{2,1,0:T(8,128)(2,1)S(1)}, u32[]{:S(2)}, u32[]{:S(2)}) %all-to-all-start.1) | async-done | bytes 852000 | tf_op jit(solution)/shard_map/all_to_all | solution.py:876
  69.0 5.9 %all-to-all-start.2 = ((s16[16,272,128]{2,1,0:T(8,128)(2,1)}), s16[16,272,128]{2,1,0:T(8,128)(2,1)}, u32[]{:S(2)}, u32[]{:S(2)}) async-start(s16[16,272,128]{2,1,0:T(8,128)(2,1)} %get-tuple-element.56), calls=%async_computation.2 | async-start | bytes 2228224 | tf_op jit(solution)/shard_map/all_to_all | solution.py:876
  74.9 0.8 collective-permute-start.8
  75.9 1.1 collective-permute-start.4
  77.0 2.7 %collective-permute-start.5 = (bf16[64,128]{1,0:T(8,128)(2,1)S(1)}, bf16[64,128]{1,0:T(8,128)(2,1)S(1)}, u32[]{:S(2)}, u32[]{:S(2)}) collective-permute-start(bf16[64,128]{1,0:T(8,128)(2,1)S(1)} %get-tuple-element.46), channel_id=1, source_target_pairs={{0,4},{1,5},{2,6},{3,7},{4,0},{5,1},{6,2},{7,3},{8,12},{9,13},{10,... | collective-permute-start | bytes 49160 | tf_op jit(solution)/shard_map/ppermute | solution.py:917
  79.7 1.0 collective-permute-start.6
  80.7 4.5 %collective-permute-done.8.refs_6_ = bf16[304,512]{1,0:T(8,128)(2,1)S(1)} collective-permute-done((bf16[304,512]{1,0:T(8,128)(2,1)S(1)}, bf16[304,512]{1,0:T(8,128)(2,1)S(1)}, u32[]{:S(2)}, u32[]{:S(2)}) %collective-permute-start.8) | collective-permute-done | bytes 311328 | tf_op jit(solution)/shard_map/ppermute | solution.py:884
  87.4 2.1 %collective-permute-done.13.other_ref = bf16[128,128]{1,0:T(8,128)(2,1)S(1)} collective-permute-done((bf16[128,128]{1,0:T(8,128)(2,1)S(1)}, bf16[128,128]{1,0:T(8,128)(2,1)S(1)}, u32[]{:S(2)}, u32[]{:S(2)}) %collective-permute-start.13) | collective-permute-done | bytes 32800 | tf_op jit(solution)/shard_map/ppermute | solution.py:889
  89.5 3.3 %all-to-all-done.2.got_ref = s16[16,272,128]{2,1,0:T(8,128)(2,1)} async-done(((s16[16,272,128]{2,1,0:T(8,128)(2,1)}), s16[16,272,128]{2,1,0:T(8,128)(2,1)}, u32[]{:S(2)}, u32[]{:S(2)}) %all-to-all-start.2) | async-done | bytes 1114144 | tf_op jit(solution)/shard_map/all_to_all | solution.py:876
  92.8 2.9 %pack_sums.1 = bf16[16,448,128]{2,1,0:T(8,128)(2,1)} custom-call(s16[16,272,128]{2,1,0:T(8,128)(2,1)} %all-to-all-done.2.got_ref, bf16[128,128]{1,0:T(8,128)(2,1)} %copy-done.4, bf16[128,128]{1,0:T(8,128)(2,1)} %copy-done.10), custom_call_target="tpu_custom_call" | custom-call | flops 1048576 | bytes 3145728 | tf_op jit(solution)/shard_map/pack_sums/pallas_call | solution.py:687
  95.8 4.2 %all-to-all-start.3 = ((bf16[16,448,128]{2,1,0:T(8,128)(2,1)}), bf16[16,448,128]{2,1,0:T(8,128)(2,1)S(1)}, u32[]{:S(2)}, u32[]{:S(2)}) async-start(bf16[16,448,128]{2,1,0:T(8,128)(2,1)} %pack_sums.1), calls=%async_computation.3 | async-start | bytes 3670016 | tf_op jit(solution)/shard_map/all_to_all | solution.py:876
  100.0 1.2 copy-done.7
  101.2 14.0 %byte_grads.1 = (bf16[4096,128]{1,0:T(8,128)(2,1)}, f32[16,128]{1,0:T(8,128)S(1)}, f32[16,128]{1,0:T(8,128)S(1)}) custom-call(s32[1]{0:T(128)} %bitcast.member, s32[8]{0:T(128)S(1)} %copy-done.9, bf16[4,304,512]{2,1,0:T(8,128)(2,1)} %copy-done.5, bf16[4,304,512]{2,1,0:T(8,128)(2,1)} %collective-permute-done.10.other_hbm, bf16[1024,512]{1,0:T(8,128)(2,1)S(1)} %copy-done.7, ...), custom_call_target="tpu_custom_call" | custom-call | flops 8589934592 | bytes 8388608 | tf_op jit(solution)/shard_map/byte_grads/pallas_call | solution.py:842
  115.2 3.9 %collective-permute-start.11 = (f32[16,128]{1,0:T(8,128)S(1)}, f32[16,128]{1,0:T(8,128)S(1)}, u32[]{:S(2)}, u32[]{:S(2)}) collective-permute-start(f32[16,128]{1,0:T(8,128)S(1)} %get-tuple-element.53), channel_id=1, source_target_pairs={{0,8},{8,16},{16,24},{24,32},{32,40},{40,48},{48,56},{56,64},{64,7... | collective-permute-start | bytes 24584 | tf_op jit(solution)/shard_map/ppermute | solution.py:872
  119.1 5.6 %collective-permute-done.11 = f32[16,128]{1,0:T(8,128)S(1)} collective-permute-done((f32[16,128]{1,0:T(8,128)S(1)}, f32[16,128]{1,0:T(8,128)S(1)}, u32[]{:S(2)}, u32[]{:S(2)}) %collective-permute-start.11) | collective-permute-done | bytes 8224 | tf_op jit(solution)/shard_map/ppermute | solution.py:872
  125.3 4.5 %all-to-all-done.3.got_ref = bf16[16,448,128]{2,1,0:T(8,128)(2,1)S(1)} async-done(((bf16[16,448,128]{2,1,0:T(8,128)(2,1)}), bf16[16,448,128]{2,1,0:T(8,128)(2,1)S(1)}, u32[]{:S(2)}, u32[]{:S(2)}) %all-to-all-start.3) | async-done | bytes 1835040 | tf_op jit(solution)/shard_map/all_to_all | solution.py:876
  129.9 2.0 %unpack_sums.1 = (f32[3,128,1024]{2,1,0:T(8,128)}, f32[1024,512]{1,0:T(8,128)}) custom-call(s32[1]{0:T(128)} %bitcast.member, bf16[16,448,128]{2,1,0:T(8,128)(2,1)S(1)} %all-to-all-done.3.got_ref), custom_call_target="tpu_custom_call" | custom-call | flops 1048576 | bytes 6291456 | tf_op jit(solution)/shard_map/unpack_sums/pallas_call | solution.py:733
  (41 shorter events, 4.1 us)
Async XLA Ops:
  1.4 5.8 %collective-permute-start = (bf16[16,1024]{1,0:T(8,128)(2,1)S(1)}, bf16[16,1024]{1,0:T(8,128)(2,1)S(1)}, u32[]{:S(2)}, u32[]{:S(2)}) collective-permute-start(bf16[16,1024]{1,0:T(8,128)(2,1)S(1)} %slice.3), channel_id=1, source_target_pairs={{8,0},{16,8},{24,16},{32,24},{40,32},{48,40},{56,48},{64,56},{72,6... | collective-permute-start | bytes 98312 | tf_op jit(solution)/shard_map/ppermute | solution.py:872
  7.2 6.1 %copy-start.11 = (bf16[16,1024]{1,0:T(8,128)(2,1)}, bf16[16,1024]{1,0:T(8,128)(2,1)S(1)}, u32[]{:S(2)}) copy-start(bf16[16,1024]{1,0:T(8,128)(2,1)S(1)} %collective-permute-done.rim_ref) | copy-start | bytes 98308
  7.2 26.2 %all-to-all-start = ((s16[8,144,512]{2,1,0:T(8,128)(2,1)}), s16[8,144,512]{2,1,0:T(8,128)(2,1)S(1)}, u32[]{:S(2)}, u32[]{:S(2)}) async-start(s16[8,144,512]{2,1,0:T(8,128)(2,1)} %att_grad.1), calls=%async_computation | async-start | bytes 2359296 | tf_op jit(solution)/shard_map/all_to_all | solution.py:876
  28.4 16.9 %collective-permute-start.3 = (bf16[128,512]{1,0:T(8,128)(2,1)}, bf16[128,512]{1,0:T(8,128)(2,1)S(1)}, u32[]{:S(2)}, u32[]{:S(2)}) collective-permute-start(bf16[128,512]{1,0:T(8,128)(2,1)} %get-tuple-element.54.refs_0_), channel_id=1, source_target_pairs={{0,6},{1,7},{2,0},{3,1},{4,2},{5,3},{6,4},{7,5},{8,14},{9,15},{10,... | collective-permute-start | bytes 393224 | tf_op jit(solution)/shard_map/ppermute | solution.py:884
  31.7 13.7 %collective-permute-start.2 = (bf16[128,512]{1,0:T(8,128)(2,1)}, bf16[128,512]{1,0:T(8,128)(2,1)S(1)}, u32[]{:S(2)}, u32[]{:S(2)}) collective-permute-start(bf16[128,512]{1,0:T(8,128)(2,1)} %get-tuple-element.54.refs_0_), channel_id=1, source_target_pairs={{0,4},{1,5},{2,6},{3,7},{4,0},{5,1},{6,2},{7,3},{8,12},{9,13},{10,... | collective-permute-start | bytes 393224 | tf_op jit(solution)/shard_map/ppermute | solution.py:884
  32.6 12.8 %collective-permute-start.1 = (bf16[128,512]{1,0:T(8,128)(2,1)}, bf16[128,512]{1,0:T(8,128)(2,1)S(1)}, u32[]{:S(2)}, u32[]{:S(2)}) collective-permute-start(bf16[128,512]{1,0:T(8,128)(2,1)} %get-tuple-element.54.refs_0_), channel_id=1, source_target_pairs={{0,2},{1,3},{2,4},{3,5},{4,6},{5,7},{6,0},{7,1},{8,10},{9,11},{10,... | collective-permute-start | bytes 393224 | tf_op jit(solution)/shard_map/ppermute | solution.py:884
  33.7 0.7 copy-start.2
  34.4 20.1 %copy-start.3 = (bf16[128,512]{1,0:T(8,128)(2,1)S(1)}, bf16[128,512]{1,0:T(8,128)(2,1)}, u32[]{:S(2)}) copy-start(bf16[128,512]{1,0:T(8,128)(2,1)} %get-tuple-element.54.refs_0_) | copy-start | bytes 393220
  45.3 9.3 %copy-start.1 = (bf16[304,512]{1,0:T(8,128)(2,1)S(1)}, bf16[304,512]{1,0:T(8,128)(2,1)}, u32[]{:S(2)}) copy-start(bf16[304,512]{1,0:T(8,128)(2,1)} %get-tuple-element.48.refs_4_) | copy-start | bytes 933892
  45.3 11.7 %copy-start = (bf16[512,512]{1,0:T(8,128)(2,1)S(1)}, bf16[512,512]{1,0:T(8,128)(2,1)}, u32[]{:S(2)}) copy-start(bf16[512,512]{1,0:T(8,128)(2,1)} %cot_ref.3) | copy-start | bytes 1572868
  45.3 11.7 %copy-start.6 = (s32[1,512]{1,0:T(1,128)S(1)}, s32[1,512]{1,0:T(1,128)}, u32[]{:S(2)}) copy-start(s32[1,512]{1,0:T(1,128)} %owner_ref.1) | copy-start | bytes 6148
  45.4 23.6 %all-to-all-start.1 = ((s16[16,208,128]{2,1,0:T(8,128)(2,1)}), s16[16,208,128]{2,1,0:T(8,128)(2,1)S(1)}, u32[]{:S(2)}, u32[]{:S(2)}) async-start(s16[16,208,128]{2,1,0:T(8,128)(2,1)} %get-tuple-element.43), calls=%async_computation.1 | async-start | bytes 1703936 | tf_op jit(solution)/shard_map/all_to_all | solution.py:876
  54.5 2.5 %collective-permute-start.12 = (bf16[4,128,512]{2,1,0:T(8,128)(2,1)S(1)}, bf16[4,128,512]{2,1,0:T(8,128)(2,1)S(1)}, u32[]{:S(2)}, u32[]{:S(2)}) collective-permute-start(bf16[4,128,512]{2,1,0:T(8,128)(2,1)S(1)} %stack.1.mine_ref), channel_id=1, source_target_pairs={{0,1},{1,0},{2,3},{3,2},{4,5},{5,4},{6,7},{7,6},{8,9},{9,8},{10,11... | collective-permute-start | bytes 1572872 | tf_op jit(solution)/shard_map/ppermute | solution.py:889
  54.6 9.8 %collective-permute-start.9 = (bf16[304,512]{1,0:T(8,128)(2,1)S(1)}, bf16[304,512]{1,0:T(8,128)(2,1)S(1)}, u32[]{:S(2)}, u32[]{:S(2)}) collective-permute-start(bf16[304,512]{1,0:T(8,128)(2,1)S(1)} %copy-done.1), channel_id=1, source_target_pairs={{0,6},{1,7},{2,0},{3,1},{4,2},{5,3},{6,4},{7,5},{8,14},{9,15},{10,... | collective-permute-start | bytes 933896 | tf_op jit(solution)/shard_map/ppermute | solution.py:884
  57.0 10.6 %collective-permute-start.7 = (bf16[304,512]{1,0:T(8,128)(2,1)S(1)}, bf16[304,512]{1,0:T(8,128)(2,1)S(1)}, u32[]{:S(2)}, u32[]{:S(2)}) collective-permute-start(bf16[304,512]{1,0:T(8,128)(2,1)S(1)} %copy-done.1), channel_id=1, source_target_pairs={{0,2},{1,3},{2,4},{3,5},{4,6},{5,7},{6,0},{7,1},{8,10},{9,11},{10,... | collective-permute-start | bytes 933896 | tf_op jit(solution)/shard_map/ppermute | solution.py:884
  69.0 23.8 %all-to-all-start.2 = ((s16[16,272,128]{2,1,0:T(8,128)(2,1)}), s16[16,272,128]{2,1,0:T(8,128)(2,1)}, u32[]{:S(2)}, u32[]{:S(2)}) async-start(s16[16,272,128]{2,1,0:T(8,128)(2,1)} %get-tuple-element.56), calls=%async_computation.2 | async-start | bytes 2228224 | tf_op jit(solution)/shard_map/all_to_all | solution.py:876
  74.9 10.3 %collective-permute-start.8 = (bf16[304,512]{1,0:T(8,128)(2,1)S(1)}, bf16[304,512]{1,0:T(8,128)(2,1)S(1)}, u32[]{:S(2)}, u32[]{:S(2)}) collective-permute-start(bf16[304,512]{1,0:T(8,128)(2,1)S(1)} %copy-done.1), channel_id=1, source_target_pairs={{0,4},{1,5},{2,6},{3,7},{4,0},{5,1},{6,2},{7,3},{8,12},{9,13},{10,... | collective-permute-start | bytes 933896 | tf_op jit(solution)/shard_map/ppermute | solution.py:884
  75.9 9.3 %collective-permute-start.4 = (bf16[64,128]{1,0:T(8,128)(2,1)S(1)}, bf16[64,128]{1,0:T(8,128)(2,1)S(1)}, u32[]{:S(2)}, u32[]{:S(2)}) collective-permute-start(bf16[64,128]{1,0:T(8,128)(2,1)S(1)} %get-tuple-element.45), channel_id=1, source_target_pairs={{0,2},{1,3},{2,0},{3,1},{4,6},{5,7},{6,4},{7,5},{8,10},{9,11},{10,... | collective-permute-start | bytes 49160 | tf_op jit(solution)/shard_map/ppermute | solution.py:917
  77.0 8.5 %collective-permute-start.5 = (bf16[64,128]{1,0:T(8,128)(2,1)S(1)}, bf16[64,128]{1,0:T(8,128)(2,1)S(1)}, u32[]{:S(2)}, u32[]{:S(2)}) collective-permute-start(bf16[64,128]{1,0:T(8,128)(2,1)S(1)} %get-tuple-element.46), channel_id=1, source_target_pairs={{0,4},{1,5},{2,6},{3,7},{4,0},{5,1},{6,2},{7,3},{8,12},{9,13},{10,... | collective-permute-start | bytes 49160 | tf_op jit(solution)/shard_map/ppermute | solution.py:917
  79.7 5.8 %collective-permute-start.6 = (bf16[64,128]{1,0:T(8,128)(2,1)S(1)}, bf16[64,128]{1,0:T(8,128)(2,1)S(1)}, u32[]{:S(2)}, u32[]{:S(2)}) collective-permute-start(bf16[64,128]{1,0:T(8,128)(2,1)S(1)} %get-tuple-element.47), channel_id=1, source_target_pairs={{0,6},{1,7},{2,4},{3,5},{4,2},{5,3},{6,0},{7,1},{8,14},{9,15},{10,... | collective-permute-start | bytes 49160 | tf_op jit(solution)/shard_map/ppermute | solution.py:917
  86.3 0.6 copy-start.4
  86.9 8.9 %copy-start.5 = (bf16[4,304,512]{2,1,0:T(8,128)(2,1)}, bf16[4,304,512]{2,1,0:T(8,128)(2,1)S(1)}, u32[]{:S(2)}) copy-start(bf16[4,304,512]{2,1,0:T(8,128)(2,1)S(1)} %get-tuple-element.49.mine_hbm) | copy-start | bytes 3735556
  86.9 13.0 %collective-permute-start.10 = (bf16[4,304,512]{2,1,0:T(8,128)(2,1)S(1)}, bf16[4,304,512]{2,1,0:T(8,128)(2,1)}, u32[]{:S(2)}, u32[]{:S(2)}) collective-permute-start(bf16[4,304,512]{2,1,0:T(8,128)(2,1)S(1)} %get-tuple-element.49.mine_hbm), channel_id=1, source_target_pairs={{0,1},{1,0},{2,3},{3,2},{4,5},{5,4},{6,7},{7,6},{8,9},{9,8},{10,11... | collective-permute-start | bytes 3735560 | tf_op jit(solution)/shard_map/ppermute | solution.py:889
  86.9 2.6 %collective-permute-start.13 = (bf16[128,128]{1,0:T(8,128)(2,1)S(1)}, bf16[128,128]{1,0:T(8,128)(2,1)S(1)}, u32[]{:S(2)}, u32[]{:S(2)}) collective-permute-start(bf16[128,128]{1,0:T(8,128)(2,1)S(1)} %get-tuple-element.58), channel_id=1, source_target_pairs={{0,1},{1,0},{2,3},{3,2},{4,5},{5,4},{6,7},{7,6},{8,9},{9,8},{10,11... | collective-permute-start | bytes 98312 | tf_op jit(solution)/shard_map/ppermute | solution.py:889
  89.5 3.3 %copy-start.10 = (bf16[128,128]{1,0:T(8,128)(2,1)}, bf16[128,128]{1,0:T(8,128)(2,1)S(1)}, u32[]{:S(2)}) copy-start(bf16[128,128]{1,0:T(8,128)(2,1)S(1)} %collective-permute-done.13.other_ref) | copy-start | bytes 98308
  95.7 4.2 %copy-start.8 = (s32[16,512]{1,0:T(8,128)S(1)}, s32[16,512]{1,0:T(8,128)}, u32[]{:S(2)}) copy-start(s32[16,512]{1,0:T(8,128)} %get-tuple-element.40.row_ref) | copy-start | bytes 98308
  95.7 4.2 %copy-start.9 = (s32[8]{0:T(128)S(1)}, s32[8]{0:T(128)}, u32[]{:S(2)}) copy-start(s32[8]{0:T(128)} %get-tuple-element.33.bounds) | copy-start | bytes 100
  95.8 34.1 %all-to-all-start.3 = ((bf16[16,448,128]{2,1,0:T(8,128)(2,1)}), bf16[16,448,128]{2,1,0:T(8,128)(2,1)S(1)}, u32[]{:S(2)}, u32[]{:S(2)}) async-start(bf16[16,448,128]{2,1,0:T(8,128)(2,1)} %pack_sums.1), calls=%async_computation.3 | async-start | bytes 3670016 | tf_op jit(solution)/shard_map/all_to_all | solution.py:876
  100.0 1.2 copy-start.7
  115.2 9.5 %collective-permute-start.11 = (f32[16,128]{1,0:T(8,128)S(1)}, f32[16,128]{1,0:T(8,128)S(1)}, u32[]{:S(2)}, u32[]{:S(2)}) collective-permute-start(f32[16,128]{1,0:T(8,128)S(1)} %get-tuple-element.53), channel_id=1, source_target_pairs={{0,8},{8,16},{16,24},{24,32},{32,40},{40,48},{48,56},{56,64},{64,7... | collective-permute-start | bytes 24584 | tf_op jit(solution)/shard_map/ppermute | solution.py:872
